TPU v7x, 512 devices: a whole 4x4x16 slice. The times are simulated.
512 devices in a mesh: replica: 32 (over x_hi, z), fsdp: 16 (over y, x_lo, core).
Axes of the slice: x: 4 (x_hi: 2, x_lo: 2; x = x_hi * 2 + x_lo), y: 4, z: 16, core: 2. Of those that a mesh axis runs over, the one named last changes fastest.
Arguments:
- activations: bfloat16 [32, 2048, 4096], P('replica', 'fsdp'), may hold values from -6 to 6
- cotangent: bfloat16 [32, 2048, 512], P('replica', 'fsdp'), may hold values from -6 to 6
- master: float32 [32, 4096, 512], P('replica', 'fsdp'), may hold values from -6 to 6
- moment_one: float32 [32, 4096, 512], P('replica', 'fsdp'), may hold values from -4 to 4
- moment_two: float32 [32, 4096, 512], P('replica', 'fsdp'), may hold values from 0.001 to 1
- lengths: int32 [32, 16], P('replica'), may hold values from 1 to 128, 1536 in all within a row
- pseudo_grad: float32 [32, 16, 256, 512], P('replica', 'fsdp'), may hold values from -8 to 8
- anchor: float32 [16, 256, 512], P('fsdp', 'replica'), may hold values from -6 to 6
- momentum: float32 [16, 256, 512], P('fsdp', 'replica'), may hold values from -4 to 4
Outputs:
- input_grad: bfloat16 [32, 2048, 4096], P('replica', 'fsdp')
- master_out: float32 [32, 4096, 512], P('replica', 'fsdp')
- fragment_weights: bfloat16 [16, 256, 512], P('fsdp')
- anchor_out: float32 [16, 256, 512], P('fsdp', 'replica')
- momentum_out: float32 [16, 256, 512], P('fsdp', 'replica')
Inputs may be any that keep to these rules, and one draw needn't show every extreme that they name: In each replica the 16 lengths sum to 1536 and one of them is exactly 128.
All inputs are finite; a program needn't handle non-finite values.
Results may differ from a plain program's by a relative error of at most 0.02.
Values may be sent and summed in bfloat16 or wider, within the bound.
No kernel may reach another device: no remote copies, remote signals or barrier semaphores. Data moves between devices by JAX's collectives and lax.ppermute only.
A program may use at most 64 MiB of HBM per device.

v0:
```python
import math

import jax
import jax.numpy as jnp
from jax import lax
from jax.sharding import PartitionSpec as P


def local(
    activations, cotangent, master, moment_one, moment_two, lengths, pseudo_grad, anchor, momentum
):
    fsdp_index = lax.axis_index("fsdp")
    tok_count = activations.shape[1]
    width = activations.shape[2]
    factor = 1.0 / math.sqrt(width)
    own_length = jnp.sum(jnp.where(jnp.arange(lengths.shape[1]) == fsdp_index, lengths[0], 0))
    alive = jnp.arange(tok_count) < own_length
    masked = jnp.where(alive[:, None], cotangent[0], jnp.zeros((), cotangent.dtype))
    weights_half = master[0].astype(jnp.bfloat16)
    gathered_grad = lax.dot_general(
        masked,
        lax.all_gather(weights_half, "fsdp", axis=0, tiled=True),
        (((1,), (1,)), ((), ())),
        preferred_element_type=jnp.float32,
    )
    input_grad = (gathered_grad * factor).astype(jnp.bfloat16)
    features = activations[0]
    term = lax.dot_general(
        features, masked, (((0,), (0,)), ((), ())), preferred_element_type=jnp.float32
    )
    summed = lax.psum_scatter(
        lax.optimization_barrier(term.astype(jnp.bfloat16))
        .astype(jnp.float32)
        .astype(jnp.bfloat16),
        "fsdp",
        scatter_dimension=0,
        tiled=True,
    ).astype(jnp.float32)
    grad = summed * factor
    first = 0.9 * moment_one[0] + 0.1 * grad
    second = 0.95 * moment_two[0] + 0.05 * grad * grad
    master_out = master[0] * (1.0 - 0.1 * 0.1) - 0.1 * first / (jnp.sqrt(second) + 1e-08)
    share_rows = anchor.shape[1]
    replica_count = lax.axis_size("replica")
    everything = lax.psum(pseudo_grad[0, 0].astype(jnp.bfloat16), "replica").astype(jnp.float32)
    own_sum = lax.dynamic_slice_in_dim(
        everything, lax.axis_index("replica") * share_rows, share_rows, 0
    )
    delta = own_sum / replica_count
    momentum_out = 0.9 * momentum[0] + delta
    anchor_out = anchor[0] - 0.7 * (delta + 0.9 * momentum_out)
    fresh = lax.all_gather(anchor_out.astype(jnp.bfloat16), "replica", axis=0, tiled=True)
    return (input_grad[None], master_out[None], fresh[None], anchor_out[None], momentum_out[None])


def solution(mesh):
    placed = (
        P("replica", "fsdp", None),
        P("replica", "fsdp", None),
        P("replica", "fsdp", None),
        P("replica", "fsdp", None),
        P("replica", "fsdp", None),
        P("replica", None),
        P("replica", "fsdp", None, None),
        P("fsdp", "replica", None),
        P("fsdp", "replica", None),
    )
    return jax.shard_map(
        local,
        mesh=mesh,
        in_specs=placed,
        out_specs=(
            P("replica", "fsdp", None),
            P("replica", "fsdp", None),
            P("fsdp", None, None),
            P("fsdp", "replica", None),
            P("fsdp", "replica", None),
        ),
        check_vma=False,
    )
```

profile of v0, /device:TPU:8, one launch (start us, length us, event | category | flops | bytes accessed | tf_op | source)
XLA Modules:
  0.0 407.3 jit_solution(1886258219294162015)
XLA Ops:
  8.0 0.0 copy-start
  8.0 0.0 all-reduce.2.cloned.1.call-start
  8.1 1.9 convert_bitcast_fusion
  9.9 0.0 all-reduce.2.cloned.1.call-update
  9.9 0.0 all-gather.3.cloned.1.call-start
  10.0 1.8 convert_element_type.32
  11.8 0.0 all-gather.3.cloned.1.call-update
  11.8 0.0 reduce-scatter.2.cloned.1.call-start
  11.8 1.3 fusion.21
  13.1 0.6 iota_compare_fusion
  13.8 4.3 %fusion = bf16[4096,512]{0,1:T(8,128)(2,1)} fusion(bf16[1,128,4096]{2,1,0:T(8,128)(2,1)S(1)} %copy-done, bf16[1,128,512]{2,1,0:T(8,128)(2,1)} %param.10, pred[128]{0:T(512)(128)(4,1)S(1)} %iota_compare_fusion), kind=kOutput, calls=%fused_computation.1 | convolution fusion | flops 539033600 | bytes 5374080 | tf_op jit(solution)/shard_map/dot_general | solution.py:28
  18.1 0.0 copy-start.2
  18.1 0.0 reduce-scatter.2.cloned.1.call-update
  18.2 0.2 copy.14
  18.4 0.8 copy-done.3
  19.2 0.2 copy.16
  19.4 0.2 copy.15
  19.6 295.2 %all-reduce.2.cloned.1.call-done = bf16[256,512]{1,0:T(8,128)(2,1)} async-done(((bf16[256,512]{1,0:T(8,128)(2,1)}), bf16[256,512]{1,0:T(8,128)(2,1)}) %all-reduce.2.cloned.1.call-update) | async-done | bytes 262160 | tf_op jit(solution)/shard_map/psum | solution.py:45
  314.8 1.3 fusion.24
  316.1 76.1 %all_gather.7 = bf16[256,512]{1,0:T(8,128)(2,1)S(1)} all-gather(bf16[8,512]{1,0:T(8,128)(2,1)S(1)} %get-tuple-element.11), channel_id=1, replica_groups=mesh['replica'=32,'fsdp'=16] {'replica'}, dimensions={0}, use_global_device_ids=true | all-gather | bytes 270336 | tf_op jit(solution)/shard_map/all_gather | solution.py:52
  392.2 4.7 %fusion.2 = bf16[1,128,4096]{2,1,0:T(8,128)(2,1)} fusion(bf16[1,4096,512]{2,1,0:T(8,128)(2,1)} %all-gather.3.cloned.1.call-done, bf16[1,128,512]{2,1,0:T(8,128)(2,1)S(1)} %copy-done.2, pred[128]{0:T(512)(128)(4,1)S(1)} %iota_compare_fusion), kind=kOutput, calls=%fused_computation.4 | convolution fusion | flops 537985024 | bytes 5374080 | tf_op jit(solution)/shard_map/dot_general | solution.py:20
  396.8 1.3 fusion.9
  398.2 1.0 copy.17
  399.2 0.7 copy.20
  (13 shorter events, 0.0 us)
Async XLA Ops:
  8.0 5.8 %copy-start = (bf16[1,128,4096]{2,1,0:T(8,128)(2,1)S(1)}, bf16[1,128,4096]{2,1,0:T(8,128)(2,1)}, u32[]{:S(2)}) copy-start(bf16[1,128,4096]{2,1,0:T(8,128)(2,1)} %param.9) | copy-start | bytes 3145732
  8.0 306.7 %all-reduce.2.cloned.1.call-start = ((), (), s32[]{:S(2)}) async-start(), calls=%async_computation.2 | async-start | bytes 524288 | tf_op jit(solution)/shard_map/psum | solution.py:45
  9.9 382.2 %all-gather.3.cloned.1.call-start = ((), (), s32[]{:S(2)}) async-start(), calls=%async_computation.3 | async-start | bytes 4456448 | tf_op jit(solution)/shard_map/all_gather | solution.py:22
  11.8 385.0 %reduce-scatter.2.cloned.1.call-start = ((), (), s32[]{:S(2)}) async-start(), calls=%async_computation.1 | async-start | bytes 4456448 | tf_op jit(solution)/shard_map/reduce_scatter | solution.py:31
  13.8 4.4 %copy-start.1 = (f32[1,256,512]{2,1,0:T(8,128)S(1)}, f32[1,256,512]{2,1,0:T(8,128)}, u32[]{:S(2)}) copy-start(f32[1,256,512]{2,1,0:T(8,128)} %param.11) | copy-start | bytes 1572868
  18.1 1.0 copy-start.3
  18.1 1.2 copy-start.4
  18.1 296.6 %copy-start.5 = (f32[1,8,512]{2,1,0:T(8,128)S(1)}, f32[1,8,512]{2,1,0:T(8,128)}, u32[]{:S(2)}) copy-start(f32[1,8,512]{2,1,0:T(8,128)} %param.17) | copy-start | bytes 49156
  18.1 296.6 %copy-start.6 = (f32[1,8,512]{2,1,0:T(8,128)S(1)}, f32[1,8,512]{2,1,0:T(8,128)}, u32[]{:S(2)}) copy-start(f32[1,8,512]{2,1,0:T(8,128)} %param.16) | copy-start | bytes 49156
  18.1 374.0 %copy-start.2 = (bf16[1,128,512]{2,1,0:T(8,128)(2,1)S(1)}, bf16[1,128,512]{2,1,0:T(8,128)(2,1)}, u32[]{:S(2)}) copy-start(bf16[1,128,512]{2,1,0:T(8,128)(2,1)} %param.10) | copy-start | bytes 393220
Sparse Core Ops, SparseCore 0:
  12.3 302.3 all-reduce.1
Sparse Core Ops, SparseCore 1:
  13.1 49.4 all-gather.2
  65.3 71.3 reduce-scatter.1
where the time goes:
time: 408 us; the launch traced here: 407 us
  waiting for transfers between devices  295 us (72%)
  blocking collectives  76.1 us (19%)
  between operations  15.6 us (4%)
  matrix products  8.94 us (2%)
  other arithmetic  8.22 us (2%)
    psum x1, waiting for transfers between devices, local(): lax.psum(pseudo_grad[0, 0].astype(jnp.bfloat16), 'replica')  295 us
    all_gather x1, blocking collectives, local(): lax.all_gather(anchor_out.astype(jnp.bfloat16), 'replica', axis=0, tiled=...  76.1 us
  transfers between devices with their start and end apart: 3, of which 1 were waited for; matrix products, arithmetic and copies ran while one was open for 4% of the time, Pallas kernels for 0%

commit v1 on v0

v1 whole, which is shorter than its diff:
```python
import math

import jax
import jax.numpy as jnp
from jax import lax
from jax.sharding import PartitionSpec as P


def local(
    activations, cotangent, master, moment_one, moment_two, lengths, pseudo_grad, anchor, momentum
):
    shards = lax.axis_size("fsdp")
    replicas = lax.axis_size("replica")
    fsdp_index = lax.axis_index("fsdp")
    tok_count = activations.shape[1]
    width = activations.shape[2]
    share_rows = anchor.shape[1]
    factor = 1.0 / math.sqrt(width)

    pieces = pseudo_grad[0, 0].astype(jnp.bfloat16).reshape(replicas, share_rows, -1)
    pieces = lax.all_to_all(pieces, "replica", 0, 0)
    delta = jnp.sum(pieces.astype(jnp.float32), axis=0) / replicas
    momentum_out = 0.9 * momentum[0] + delta
    anchor_out = anchor[0] - 0.7 * (delta + 0.9 * momentum_out)
    fresh = jnp.broadcast_to(anchor_out.astype(jnp.bfloat16)[None], pieces.shape)
    fresh = lax.all_to_all(fresh, "replica", 0, 0).reshape(pseudo_grad.shape[2:])

    own_length = lax.dynamic_index_in_dim(lengths[0], fsdp_index, keepdims=False)
    alive = jnp.arange(tok_count) < own_length
    masked = jnp.where(alive[:, None], cotangent[0], jnp.zeros((), cotangent.dtype))
    weights = lax.all_gather(master[0].astype(jnp.bfloat16), "fsdp", axis=0, tiled=True)
    everyone = lax.all_gather(masked, "fsdp", axis=0, tiled=True)

    features = lax.all_to_all(activations[0], "fsdp", 1, 0, tiled=True)
    summed = lax.dot_general(
        features, everyone, (((0,), (0,)), ((), ())), preferred_element_type=jnp.float32
    )
    grad = summed * factor
    first = 0.9 * moment_one[0] + 0.1 * grad
    second = 0.95 * moment_two[0] + 0.05 * grad * grad
    master_out = master[0] * (1.0 - 0.1 * 0.1) - 0.1 * first / (jnp.sqrt(second) + 1e-08)

    input_grad = lax.dot_general(
        masked, weights, (((1,), (1,)), ((), ())), preferred_element_type=jnp.float32
    )
    input_grad = (input_grad * factor).astype(jnp.bfloat16)
    return (input_grad[None], master_out[None], fresh[None], anchor_out[None], momentum_out[None])


def solution(mesh):
    placed = (
        P("replica", "fsdp", None),
        P("replica", "fsdp", None),
        P("replica", "fsdp", None),
        P("replica", "fsdp", None),
        P("replica", "fsdp", None),
        P("replica", None),
        P("replica", "fsdp", None, None),
        P("fsdp", "replica", None),
        P("fsdp", "replica", None),
    )
    return jax.shard_map(
        local,
        mesh=mesh,
        in_specs=placed,
        out_specs=(
            P("replica", "fsdp", None),
            P("replica", "fsdp", None),
            P("fsdp", None, None),
            P("fsdp", "replica", None),
            P("fsdp", "replica", None),
        ),
        check_vma=False,
    )
```

time: 408 us -> 127 us (0.31)
  the two profiles are of different devices: /device:TPU:8 before, /device:TPU:1 now
where the time goes in v1:
time: 127 us
  waiting for transfers between devices  59.7 us (47%)
  starting transfers between devices  30.6 us (24%)
  between operations  14.2 us (11%)
  local copies, waits for them, and re-layouts  8.46 us (7%)
  matrix products  7.4 us (6%)
  other arithmetic  6.52 us (5%)
    all_to_all x1, waiting for transfers between devices, local(): pieces = lax.all_to_all(pieces, 'replica', 0, 0)  20.2 us
    all_to_all x1, starting transfers between devices, local(): pieces = lax.all_to_all(pieces, 'replica', 0, 0)  18.5 us
    all_to_all x1, waiting for transfers between devices, local(): lax.all_to_all(fresh, 'replica', 0, 0).reshape(pseudo_grad.shape[2:])  18 us
    all_to_all x1, waiting for transfers between devices, local(): features = lax.all_to_all(activations[0], 'fsdp', 1, 0, tiled=True)  15.1 us
    all_to_all x1, starting transfers between devices, local(): features = lax.all_to_all(activations[0], 'fsdp', 1, 0, tiled=True)  7.83 us
    unnamed x26, local copies, waits for them, and re-layouts  6.63 us
    all_gather x1, waiting for transfers between devices, local(): lax.all_gather(master[0].astype(jnp.bfloat16), 'fsdp', axis=0, tiled=True)  6.4 us
    dot_general x1, matrix products, local(): lax.dot_general(masked, weights, (((1,), (1,)), ((), ())), preferred_elem...  4.65 us
  transfers between devices with their start and end apart: 5, of which 4 were waited for; matrix products, arithmetic and copies ran while one was open for 11% of the time, Pallas kernels for 0%

profile of v1, /device:TPU:1, one launch (start us, length us, event | category | flops | bytes accessed | tf_op | source)
XLA Modules:
  0.0 126.8 jit_solution(13714814306073331554)
XLA Ops:
  7.2 0.6 copy-done
  7.8 0.6 constant_dynamic-slice_fusion
  8.4 0.6 iota_compare_fusion
  9.1 1.6 %bitcast_select_fusion = bf16[128,512]{1,0:T(8,128)(2,1)} fusion(bf16[1,128,512]{2,1,0:T(8,128)(2,1)} %param.10, pred[128]{0:T(512)(128)(4,1)S(1)} %iota_compare_fusion), kind=kLoop, calls=%fused_computation.14 | loop fusion | flops 65536 | bytes 262272 | tf_op jit(solution)/shard_map/jit(_where)/select_n | solution.py:30
  10.8 1.8 %convert_element_type.23 = bf16[1,256,512]{2,1,0:T(8,128)(2,1)} convert(f32[1,256,512]{2,1,0:T(8,128)} %param.11) | non-fusion elementwise | flops 131072 | bytes 786432 | tf_op jit(solution)/shard_map/convert_element_type | solution.py:31
  12.6 1.8 %convert_bitcast_fusion = bf16[32,8,512]{2,1,0:T(8,128)(2,1)} fusion(f32[1,1,256,512]{3,2,1,0:T(8,128)} %param.15), kind=kLoop, calls=%fused_computation.13 | loop fusion | flops 131072 | bytes 786432 | tf_op jit(solution)/shard_map/convert_element_type | solution.py:20
  14.4 18.5 %all-to-all-start.1 = ((bf16[32,8,512]{2,1,0:T(8,128)(2,1)}), bf16[32,8,512]{2,1,0:T(8,128)(2,1)S(1)}, u32[]{:S(2)}, u32[]{:S(2)}) async-start(bf16[32,8,512]{2,1,0:T(8,128)(2,1)} %convert_bitcast_fusion), calls=%async_computation.1 | async-start | bytes 524288 | tf_op jit(solution)/shard_map/all_to_all | solution.py:21
  32.9 1.3 %copy.24 = bf16[1,128,4096]{1,2,0:T(8,128)(2,1)} copy(bf16[1,128,4096]{2,1,0:T(8,128)(2,1)S(1)} %copy-done.3) | data formatting | bytes 2097152 | tf_op args[0]
  34.2 20.2 %all-to-all-done.1 = bf16[32,8,512]{2,1,0:T(8,128)(2,1)S(1)} async-done(((bf16[32,8,512]{2,1,0:T(8,128)(2,1)}), bf16[32,8,512]{2,1,0:T(8,128)(2,1)S(1)}, u32[]{:S(2)}, u32[]{:S(2)}) %all-to-all-start.1) | async-done | bytes 262176 | tf_op jit(solution)/shard_map/all_to_all | solution.py:21
  54.4 7.8 %all-to-all-start = ((bf16[128,16,256]{0,2,1:T(8,128)(2,1)}), bf16[128,16,256]{0,2,1:T(8,128)(2,1)S(1)}, u32[]{:S(2)}, u32[]{:S(2)}) async-start(bf16[128,16,256]{0,2,1:T(8,128)(2,1)} %bitcast.6), calls=%async_computation | async-start | bytes 2097152 | tf_op jit(solution)/shard_map/all_to_all | solution.py:34
  62.3 0.6 convert_bitcast_fusion.1
  62.9 15.1 %all-to-all-done = bf16[128,16,256]{0,2,1:T(8,128)(2,1)S(1)} async-done(((bf16[128,16,256]{0,2,1:T(8,128)(2,1)}), bf16[128,16,256]{0,2,1:T(8,128)(2,1)S(1)}, u32[]{:S(2)}, u32[]{:S(2)}) %all-to-all-start) | async-done | bytes 1048608 | tf_op jit(solution)/shard_map/all_to_all | solution.py:34
  78.0 0.7 broadcast_in_dim.34
  78.8 4.2 %all-to-all-start.2 = ((bf16[32,8,512]{2,1,0:T(8,128)(2,1)}), bf16[32,8,512]{2,1,0:T(8,128)(2,1)S(1)}, u32[]{:S(2)}, u32[]{:S(2)}) async-start(bf16[32,8,512]{2,1,0:T(8,128)(2,1)} %broadcast_in_dim.34), calls=%async_computation.2 | async-start | bytes 524288 | tf_op jit(solution)/shard_map/all_to_all | solution.py:26
  82.9 1.0 copy.22
  83.9 1.0 copy.23
  84.9 1.0 copy.26
  85.9 0.5 copy.25
  86.5 18.0 %all-to-all-done.2 = bf16[32,8,512]{2,1,0:T(8,128)(2,1)S(1)} async-done(((bf16[32,8,512]{2,1,0:T(8,128)(2,1)}), bf16[32,8,512]{2,1,0:T(8,128)(2,1)S(1)}, u32[]{:S(2)}, u32[]{:S(2)}) %all-to-all-start.2) | async-done | bytes 262176 | tf_op jit(solution)/shard_map/all_to_all | solution.py:26
  104.4 2.8 %fusion.7 = f32[1,256,512]{1,2,0:T(8,128)S(1)} fusion(f32[1,256,512]{1,2,0:T(8,128)} %copy.26, f32[1,256,512]{1,2,0:T(8,128)S(1)} %copy-done.7, f32[1,256,512]{1,2,0:T(8,128)S(1)} %copy-done.6, bf16[2048,512]{1,0:T(8,128)(2,1)} %all-gather.4.cloned.1.call-done, bf16[2048,256]{1,0:T(8,128)(2,1)S(1)} %bitcast.55), kind=kOutput, calls=%fused_computation.9 | convolution fusion | flops 538574848 | bytes 5242880 | tf_op jit(solution)/shard_map/dot_general | solution.py:35
  107.2 1.0 copy.27
  108.2 6.4 %all-gather.6.cloned.1.call-done = bf16[1,4096,512]{2,1,0:T(8,128)(2,1)} async-done(((bf16[1,256,512]{2,1,0:T(8,128)(2,1)}), bf16[1,4096,512]{2,1,0:T(8,128)(2,1)}) %all-gather.6.cloned.1.call-update) | async-done | bytes 4194320 | tf_op jit(solution)/shard_map/all_gather | solution.py:31
  114.6 4.6 %fusion.1 = bf16[1,128,4096]{2,1,0:T(8,128)(2,1)} fusion(bf16[128,512]{1,0:T(8,128)(2,1)S(1)} %copy-done.2, bf16[1,4096,512]{2,1,0:T(8,128)(2,1)} %all-gather.6.cloned.1.call-done), kind=kOutput, calls=%fused_computation.2 | convolution fusion | flops 537919488 | bytes 5373952 | tf_op jit(solution)/shard_map/dot_general | solution.py:43
  119.2 0.7 copy.29
  (25 shorter events, 0.2 us)
Async XLA Ops:
  7.2 0.7 copy-start
  7.2 25.7 %copy-start.3 = (bf16[1,128,4096]{2,1,0:T(8,128)(2,1)S(1)}, bf16[1,128,4096]{2,1,0:T(8,128)(2,1)}, u32[]{:S(2)}) copy-start(bf16[1,128,4096]{2,1,0:T(8,128)(2,1)} %param.9) | copy-start | bytes 3145732
  7.2 97.2 %all-gather.4.cloned.1.call-start = ((), (), s32[]{:S(2)}) async-start(), calls=%async_computation.3 | async-start | bytes 2228224 | tf_op jit(solution)/shard_map/all_gather | solution.py:32
  10.7 103.9 %all-gather.6.cloned.1.call-start = ((), (), s32[]{:S(2)}) async-start(), calls=%async_computation.4 | async-start | bytes 4456448 | tf_op jit(solution)/shard_map/all_gather | solution.py:31
  14.4 40.0 %all-to-all-start.1 = ((bf16[32,8,512]{2,1,0:T(8,128)(2,1)}), bf16[32,8,512]{2,1,0:T(8,128)(2,1)S(1)}, u32[]{:S(2)}, u32[]{:S(2)}) async-start(bf16[32,8,512]{2,1,0:T(8,128)(2,1)} %convert_bitcast_fusion), calls=%async_computation.1 | async-start | bytes 524288 | tf_op jit(solution)/shard_map/all_to_all | solution.py:21
  32.9 29.4 %copy-start.8 = (f32[1,8,512]{2,1,0:T(8,128)S(1)}, f32[1,8,512]{2,1,0:T(8,128)}, u32[]{:S(2)}) copy-start(f32[1,8,512]{2,1,0:T(8,128)} %param.16) | copy-start | bytes 49156
  32.9 29.4 %copy-start.9 = (f32[1,8,512]{2,1,0:T(8,128)S(1)}, f32[1,8,512]{2,1,0:T(8,128)}, u32[]{:S(2)}) copy-start(f32[1,8,512]{2,1,0:T(8,128)} %param.17) | copy-start | bytes 49156
  34.2 48.7 %copy-start.1 = (f32[1,256,512]{2,1,0:T(8,128)S(1)}, f32[1,256,512]{2,1,0:T(8,128)}, u32[]{:S(2)}) copy-start(f32[1,256,512]{2,1,0:T(8,128)} %param.11) | copy-start | bytes 1572868
  54.4 29.6 %copy-start.4 = (f32[1,256,512]{2,1,0:T(8,128)S(1)}, f32[1,256,512]{2,1,0:T(8,128)}, u32[]{:S(2)}) copy-start(f32[1,256,512]{2,1,0:T(8,128)} %param.12) | copy-start | bytes 1572868
  54.4 23.7 %all-to-all-start = ((bf16[128,16,256]{0,2,1:T(8,128)(2,1)}), bf16[128,16,256]{0,2,1:T(8,128)(2,1)S(1)}, u32[]{:S(2)}, u32[]{:S(2)}) async-start(bf16[128,16,256]{0,2,1:T(8,128)(2,1)} %bitcast.6), calls=%async_computation | async-start | bytes 2097152 | tf_op jit(solution)/shard_map/all_to_all | solution.py:34
  62.2 22.7 %copy-start.5 = (f32[1,256,512]{2,1,0:T(8,128)S(1)}, f32[1,256,512]{2,1,0:T(8,128)}, u32[]{:S(2)}) copy-start(f32[1,256,512]{2,1,0:T(8,128)} %param.13) | copy-start | bytes 1572868
  78.8 25.7 %all-to-all-start.2 = ((bf16[32,8,512]{2,1,0:T(8,128)(2,1)}), bf16[32,8,512]{2,1,0:T(8,128)(2,1)S(1)}, u32[]{:S(2)}, u32[]{:S(2)}) async-start(bf16[32,8,512]{2,1,0:T(8,128)(2,1)} %broadcast_in_dim.34), calls=%async_computation.2 | async-start | bytes 524288 | tf_op jit(solution)/shard_map/all_to_all | solution.py:26
  84.9 19.5 %copy-start.6 = (f32[1,256,512]{1,2,0:T(8,128)S(1)}, f32[1,256,512]{1,2,0:T(8,128)}, u32[]{:S(2)}) copy-start(f32[1,256,512]{1,2,0:T(8,128)} %copy.22) | copy-start | bytes 1572868
  85.9 18.5 %copy-start.7 = (f32[1,256,512]{1,2,0:T(8,128)S(1)}, f32[1,256,512]{1,2,0:T(8,128)}, u32[]{:S(2)}) copy-start(f32[1,256,512]{1,2,0:T(8,128)} %copy.23) | copy-start | bytes 1572868
  104.4 10.2 %copy-start.2 = (bf16[128,512]{1,0:T(8,128)(2,1)S(1)}, bf16[128,512]{1,0:T(8,128)(2,1)}, u32[]{:S(2)}) copy-start(bf16[128,512]{1,0:T(8,128)(2,1)} %bitcast_select_fusion) | copy-start | bytes 393220
Sparse Core Ops, SparseCore 0:
  10.9 47.8 all-gather.3
  61.5 53.0 all-gather.5

commit v2 on v1

v2 whole, which is shorter than its diff:
```python
import math

import jax
import jax.numpy as jnp
from jax import lax
from jax.experimental import pallas as pl
from jax.experimental.pallas import tpu as pltpu
from jax.sharding import PartitionSpec as P

QUAD = 4
COLUMN = 4
HALF = jnp.bfloat16
FULL = jnp.float32
SMEM = pl.BlockSpec(memory_space=pltpu.SMEM)
VMEM = pl.BlockSpec(memory_space=pltpu.VMEM)
AC_A2A = False
OUT_A2A = False


def block_of(place, step):
    return place ^ (((step & 1) << 1) | (step >> 1))


def pack_kernel(info, features, cotangent, *packed):
    block = features.shape[1] // (COLUMN * QUAD)
    row = lax.broadcasted_iota(jnp.int32, cotangent.shape, 0)
    masked = jnp.where(row < info[0], cotangent[...], jnp.zeros((), cotangent.dtype))
    for d in range(COLUMN):
        out = packed[0].at[d] if AC_A2A else packed[d]
        y = d if AC_A2A else (info[2] + d) % COLUMN
        for step in range(QUAD):
            source = pl.multiple_of((y * QUAD + block_of(info[1], step)) * block, block)
            out[:, step * block : (step + 1) * block] = features[:, pl.ds(source, block)]
        out[:, QUAD * block :] = masked


def unpack_kernel(info, *refs):
    pieces, result = refs[:-1], refs[-1]
    block = result.shape[1] // (COLUMN * QUAD)
    for d in range(COLUMN):
        piece = pieces[0].at[d] if OUT_A2A else pieces[d]
        y = d if OUT_A2A else (info[2] + d) % COLUMN
        for step in range(QUAD):
            target = pl.multiple_of((y * QUAD + block_of(info[1], step)) * block, block)
            result[:, pl.ds(target, block)] = piece[:, step * block : (step + 1) * block]


def input_kernel(factor, info, own, beside, across, *refs):
    count = 1 if AC_A2A else COLUMN
    cotangents, results = refs[:count], refs[count:]
    tokens, keys = cotangents[0].shape[-2:]
    block = own.shape[0]
    rights = (own[...], beside[...], across[:block], across[block:])
    lefts = []
    for d in range(COLUMN):
        lefts.append(cotangents[0][(info[2] + COLUMN - d) % COLUMN] if AC_A2A else cotangents[d][...])
    left = jnp.concatenate(lefts, axis=0)
    for step, right in enumerate(rights):
        product = lax.dot_general(left, right, (((1,), (1,)), ((), ())), preferred_element_type=FULL)
        product = (product * factor).astype(HALF)
        for d in range(COLUMN):
            part = product[d * tokens : (d + 1) * tokens]
            if OUT_A2A:
                results[0][(info[2] + COLUMN - d) % COLUMN, :, step * block : (step + 1) * block] = part
            else:
                results[d][:, step * block : (step + 1) * block] = part


def weight_kernel(*refs):
    count = 1 if AC_A2A else COLUMN
    packed, (kept, sent) = refs[:count], refs[count:]
    half = kept.shape[0]

    def columns(start, size):
        if AC_A2A:
            part = packed[0][:, :, start : start + size]
            return part.reshape(-1, size)
        return jnp.concatenate([ref[:, start : start + size] for ref in packed], axis=0)

    right = columns(2 * half, kept.shape[1])
    sent[...] = lax.dot_general(
        columns(half, half), right, (((0,), (0,)), ((), ())), preferred_element_type=FULL
    ).astype(HALF)
    kept[...] = lax.dot_general(
        columns(0, half), right, (((0,), (0,)), ((), ())), preferred_element_type=FULL
    )


def whole(shape):
    return pl.BlockSpec(shape, lambda *_: (0,) * len(shape))


def call(kernel, outs, ins, in_specs=None, flops=0, moved=4 << 20, grid=()):
    return pl.pallas_call(
        kernel,
        grid=grid,
        out_shape=outs,
        in_specs=in_specs,
        out_specs=jax.tree.map(lambda s: whole(s.shape), outs),
        compiler_params=pltpu.CompilerParams(vmem_limit_bytes=48 << 20),
        cost_estimate=pl.CostEstimate(flops=flops, bytes_accessed=moved, transcendentals=0),
    )(*ins)


def local(
    activations, cotangent, master, moment_one, moment_two, lengths, pseudo_grad, anchor, momentum
):
    shards = lax.axis_size("fsdp")
    replicas = lax.axis_size("replica")
    fsdp_index = lax.axis_index("fsdp")
    tokens, width = activations.shape[1:]
    keys = cotangent.shape[2]
    share_rows = anchor.shape[1]
    rows = master.shape[1]
    wide = width // COLUMN
    factor = 1.0 / math.sqrt(width)

    columns = [[QUAD * y + j for y in range(COLUMN)] for j in range(QUAD)]
    beside = [(f, f ^ 2) for f in range(shards)]
    across = [(f, f ^ 1) for f in range(shards)]
    up = [[(f, (f + QUAD * d) % shards) for f in range(shards)] for d in range(COLUMN)]
    down = [[(f, (f - QUAD * d) % shards) for f in range(shards)] for d in range(COLUMN)]
    depth = replicas // 2
    outer = depth // QUAD
    nearby = 2 * QUAD
    near = [[depth * h + QUAD * a + b for h in range(2) for b in range(QUAD)] for a in range(outer)]
    far = [[depth * h + QUAD * a + b for a in range(outer)] for h in range(2) for b in range(QUAD)]
    far_place = lax.axis_index("replica") % depth // QUAD

    pieces = pseudo_grad[0, 0].astype(HALF).reshape(2, outer, QUAD, share_rows, keys)
    pieces = pieces.transpose(0, 2, 1, 3, 4).reshape(nearby, outer * share_rows, keys)
    pieces = lax.all_to_all(pieces, "replica", 0, 0, axis_index_groups=near)

    own = master[0].astype(HALF)
    other = lax.ppermute(own, "fsdp", beside)
    both = lax.ppermute(jnp.concatenate([own, other], axis=0), "fsdp", across)

    own_length = lax.dynamic_index_in_dim(lengths[0], fsdp_index, keepdims=False)
    info = jnp.stack([own_length, fsdp_index % QUAD, fsdp_index // QUAD]).astype(jnp.int32)
    one = jax.ShapeDtypeStruct((tokens, wide + keys), HALF)
    packed_shape = jax.ShapeDtypeStruct((COLUMN, *one.shape), HALF) if AC_A2A else one
    packed = list(call(
        pack_kernel,
        [packed_shape] * (1 if AC_A2A else COLUMN),
        (info, activations[0], cotangent[0]),
        [SMEM, VMEM, VMEM],
    ))
    if AC_A2A:
        packed[0], pieces = lax.optimization_barrier((packed[0], pieces))
        packed = [lax.all_to_all(packed[0], "fsdp", 0, 0, axis_index_groups=columns)]
    else:
        packed = [packed[0]] + [lax.ppermute(packed[d], "fsdp", up[d]) for d in range(1, COLUMN)]

    pieces = jnp.sum(pieces.astype(FULL), axis=0).astype(HALF)
    base = anchor[0] - 0.7 * 0.9 * 0.9 * momentum[0]
    high = base.astype(HALF)
    low = (base - high.astype(FULL)).astype(HALF)
    pieces = jnp.concatenate([pieces, high, low], axis=0)
    pieces = jnp.broadcast_to(pieces[None], (outer, *pieces.shape))
    if AC_A2A:
        packed[0], pieces = lax.optimization_barrier((packed[0], pieces))
    pieces = lax.all_to_all(pieces, "replica", 0, 0, axis_index_groups=far)
    delta = jnp.sum(pieces[:, : outer * share_rows].astype(FULL), axis=0) / replicas
    own_delta = lax.dynamic_slice_in_dim(delta, far_place * share_rows, share_rows, 0)
    momentum_out = 0.9 * momentum[0] + own_delta
    anchor_out = anchor[0] - 0.7 * (own_delta + 0.9 * momentum_out)
    bases = pieces[:, outer * share_rows :].astype(FULL)
    bases = (bases[:, :share_rows] + bases[:, share_rows:]).reshape(delta.shape)
    fresh = (bases - 0.7 * 1.9 * delta).astype(HALF)
    fresh = jnp.broadcast_to(fresh[None], (nearby, *fresh.shape))

    cot_spec = (
        pl.BlockSpec((COLUMN, tokens, keys), lambda *_: (0, 0, wide // keys))
        if AC_A2A
        else pl.BlockSpec((tokens, keys), lambda *_: (0, wide // keys))
    )
    out = jax.ShapeDtypeStruct((tokens, wide), HALF)
    out_shape = jax.ShapeDtypeStruct((COLUMN, *out.shape), HALF) if OUT_A2A else out
    products = list(call(
        lambda *refs: input_kernel(factor, *refs),
        [out_shape] * (1 if OUT_A2A else COLUMN),
        (info, own, other, both, *packed),
        [SMEM, whole(own.shape), whole(own.shape), whole(both.shape)] + [cot_spec] * len(packed),
        2 * COLUMN * tokens * wide * keys,
        grid=(1,),
    ))
    if OUT_A2A:
        products[0], fresh = lax.optimization_barrier((products[0], fresh))
        products = [lax.all_to_all(products[0], "fsdp", 0, 0, axis_index_groups=columns)]
        products[0], fresh = lax.optimization_barrier((products[0], fresh))
    else:
        products = [products[0]] + [lax.ppermute(products[d], "fsdp", down[d]) for d in range(1, COLUMN)]
    fresh = lax.all_to_all(fresh, "replica", 0, 0, axis_index_groups=near)
    fresh = fresh.reshape(2, QUAD, outer, share_rows, keys).transpose(0, 2, 1, 3, 4)
    fresh = fresh.reshape(pseudo_grad.shape[2:])

    kept, sent = call(
        weight_kernel,
        [jax.ShapeDtypeStruct((wide // 2, keys), FULL), jax.ShapeDtypeStruct((wide // 2, keys), HALF)],
        packed,
        [VMEM] * len(packed),
        2 * COLUMN * tokens * wide * keys,
    )
    kept = kept + lax.ppermute(sent, "fsdp", across).astype(FULL)
    summed = kept[:rows] + lax.ppermute(kept[rows:].astype(HALF), "fsdp", beside).astype(FULL)

    grad = summed * factor
    first = 0.9 * moment_one[0] + 0.1 * grad
    second = 0.95 * moment_two[0] + 0.05 * grad * grad
    master_out = master[0] * (1.0 - 0.1 * 0.1) - 0.1 * first / (jnp.sqrt(second) + 1e-08)

    (input_grad,) = call(
        unpack_kernel,
        [jax.ShapeDtypeStruct((tokens, width), HALF)],
        (info, *products),
        [SMEM] + [VMEM] * len(products),
        moved=2 << 20,
    )
    return (input_grad[None], master_out[None], fresh[None], anchor_out[None], momentum_out[None])


def solution(mesh):
    placed = (
        P("replica", "fsdp", None),
        P("replica", "fsdp", None),
        P("replica", "fsdp", None),
        P("replica", "fsdp", None),
        P("replica", "fsdp", None),
        P("replica", None),
        P("replica", "fsdp", None, None),
        P("fsdp", "replica", None),
        P("fsdp", "replica", None),
    )
    return jax.shard_map(
        local,
        mesh=mesh,
        in_specs=placed,
        out_specs=(
            P("replica", "fsdp", None),
            P("replica", "fsdp", None),
            P("fsdp", None, None),
            P("fsdp", "replica", None),
            P("fsdp", "replica", None),
        ),
        check_vma=False,
    )
```

time: 127 us -> 106 us (0.83); the launches traced: 127 us -> 104 us
  waiting for transfers between devices: 59.7 us -> 27.6 us
  starting transfers between devices: 30.6 us -> 58.6 us
  between operations: 14.2 us -> 0.99 us
  matrix products: 7.4 us -> 0 us
  Pallas kernels: 0 us -> 4.98 us
  local copies, waits for them, and re-layouts: 8.46 us -> 4.66 us
    all_to_all x3, waiting for transfers between devices: 53.3 us -> 0.01 us  [the longest x1 0.01 us: local(): pieces = lax.all_to_all(pieces, 'replica', 0, 0, axis_index_groups=near)]
    ppermute x0 -> x10, starting transfers between devices: none -> 31.5 us  [the longest x3 10.7 us: local(): lax.ppermute(packed[d], 'fsdp', up[d])]
    ppermute x0 -> x10, waiting for transfers between devices: none -> 27.6 us  [the longest x3 13.6 us: local(): lax.ppermute(packed[d], 'fsdp', up[d])]
    dot_general x2 -> x0, matrix products: 7.4 us -> none  [the longest x1 4.65 us: local(): lax.dot_general(masked, weights, (((1,), (1,)), ((), ())), preferred_elem...]
    all_gather x2 -> x0, waiting for transfers between devices: 6.4 us -> none  [the longest x1 6.4 us: local(): lax.all_gather(master[0].astype(jnp.bfloat16), 'fsdp', axis=0, tiled=True)]
    unnamed x26 -> x22, local copies, waits for them, and re-layouts: 6.63 us -> 1.16 us
    pallas_call x0 -> x4, Pallas kernels: none -> 4.98 us  [call(): pl.pallas_call(kernel, grid=grid, out_shape=outs, in_specs=in_specs, out_...]
    all_to_all x3, starting transfers between devices: 30.5 us -> 27.1 us  [the longest x1 12.2 us: local(): pieces = lax.all_to_all(pieces, 'replica', 0, 0, axis_index_groups=far)]
  transfers between devices with their start and end apart: 5 -> 13, of which waited for: 4 -> 5; matrix products, arithmetic and copies ran while one was open for 11% -> 8% of each run, Pallas kernels for 0% -> 5%
where the time goes in v2:
time: 106 us; the launch traced here: 104 us
  starting transfers between devices  58.6 us (55%)
  waiting for transfers between devices  27.6 us (26%)
  other arithmetic  7.46 us (7%)
  Pallas kernels  4.98 us (5%)
  local copies, waits for them, and re-layouts  4.66 us (4%)
    ppermute x3, waiting for transfers between devices, local(): lax.ppermute(packed[d], 'fsdp', up[d])  13.6 us
    all_to_all x1, starting transfers between devices, local(): pieces = lax.all_to_all(pieces, 'replica', 0, 0, axis_index_groups=far)  12.2 us
    ppermute x3, starting transfers between devices, local(): lax.ppermute(packed[d], 'fsdp', up[d])  10.7 us
    ppermute x3, starting transfers between devices, local(): lax.ppermute(products[d], 'fsdp', down[d])  9.7 us
    all_to_all x1, starting transfers between devices, local(): pieces = lax.all_to_all(pieces, 'replica', 0, 0, axis_index_groups=near)  8.91 us
    ppermute x1, waiting for transfers between devices, local(): other = lax.ppermute(own, 'fsdp', beside)  7.77 us
    ppermute x1, waiting for transfers between devices, local(): lax.ppermute(kept[rows:].astype(HALF), 'fsdp', beside).astype(FULL)  6.19 us
    all_to_all x1, starting transfers between devices, local(): fresh = lax.all_to_all(fresh, 'replica', 0, 0, axis_index_groups=near)  5.98 us
  transfers between devices with their start and end apart: 13, of which 5 were waited for; matrix products, arithmetic and copies ran while one was open for 8% of the time, Pallas kernels for 5%

profile of v2, /device:TPU:1, one launch (start us, length us, event | category | flops | bytes accessed | tf_op | source)
XLA Modules:
  0.0 104.2 jit_solution(17344353739691053240)
XLA Ops:
  0.6 1.1 %convert_element_type.47 = bf16[1,1,256,512]{3,2,1,0:T(8,128)(2,1)S(1)} convert(f32[1,1,256,512]{3,2,1,0:T(8,128)} %param.15) | non-fusion elementwise | flops 131072 | bytes 786432 | tf_op jit(solution)/shard_map/convert_element_type | solution.py:130
  2.5 8.9 %all-to-all-start = ((bf16[8,32,512]{2,1,0:T(8,128)(2,1)}), bf16[8,32,512]{2,1,0:T(8,128)(2,1)S(1)}, u32[]{:S(2)}, u32[]{:S(2)}) async-start(bf16[8,32,512]{2,1,0:T(8,128)(2,1)} %bitcast.13), calls=%async_computation | async-start | bytes 524288 | tf_op jit(solution)/shard_map/all_to_all | solution.py:132
  11.4 2.2 %collective-permute-start = (bf16[256,512]{1,0:T(8,128)(2,1)S(1)}, bf16[256,512]{1,0:T(8,128)(2,1)S(1)}, u32[]{:S(2)}, u32[]{:S(2)}) collective-permute-start(bf16[256,512]{1,0:T(8,128)(2,1)S(1)} %convert_bitcast_fusion.refs_1_), channel_id=1, source_target_pairs={{0,2},{1,3},{2,0},{3,1},{4,6},{5,7},{6,4},{7,5},{8,10},{9,11},{10,... | collective-permute-start | bytes 786440 | tf_op jit(solution)/shard_map/ppermute | solution.py:135
  14.4 7.8 %collective-permute-done.refs_2_ = bf16[256,512]{1,0:T(8,128)(2,1)S(1)} collective-permute-done((bf16[256,512]{1,0:T(8,128)(2,1)S(1)}, bf16[256,512]{1,0:T(8,128)(2,1)S(1)}, u32[]{:S(2)}, u32[]{:S(2)}) %collective-permute-start) | collective-permute-done | bytes 262176 | tf_op jit(solution)/shard_map/ppermute | solution.py:135
  23.0 3.5 %collective-permute-start.1 = (bf16[512,512]{1,0:T(8,128)(2,1)}, bf16[512,512]{1,0:T(8,128)(2,1)S(1)}, u32[]{:S(2)}, u32[]{:S(2)}) collective-permute-start(bf16[512,512]{1,0:T(8,128)(2,1)} %pad_maximum_fusion), channel_id=1, source_target_pairs={{0,1},{1,0},{2,3},{3,2},{4,5},{5,4},{6,7},{7,6},{8,9},{9,8},{10,11... | collective-permute-start | bytes 1572872 | tf_op jit(solution)/shard_map/ppermute | solution.py:136
  27.3 12.2 %all-to-all-start.1 = ((bf16[4,48,512]{2,1,0:T(8,128)(2,1)}), bf16[4,48,512]{2,1,0:T(8,128)(2,1)}, u32[]{:S(2)}, u32[]{:S(2)}) async-start(bf16[4,48,512]{2,1,0:T(8,128)(2,1)} %broadcast_in_dim.26), calls=%async_computation.1 | async-start | bytes 393216 | tf_op jit(solution)/shard_map/all_to_all | solution.py:162
  40.9 3.2 %collective-permute-start.2 = (bf16[128,1536]{1,0:T(8,128)(2,1)S(1)}, bf16[128,1536]{1,0:T(8,128)(2,1)S(1)}, u32[]{:S(2)}, u32[]{:S(2)}) collective-permute-start(bf16[128,1536]{1,0:T(8,128)(2,1)S(1)} %get-tuple-element.16), channel_id=1, source_target_pairs={{0,4},{1,5},{2,6},{3,7},{4,8},{5,9},{6,10},{7,11},{8,12},{9,13},{1... | collective-permute-start | bytes 1179656 | tf_op jit(solution)/shard_map/ppermute | solution.py:152
  44.1 4.5 %collective-permute-start.3 = (bf16[128,1536]{1,0:T(8,128)(2,1)S(1)}, bf16[128,1536]{1,0:T(8,128)(2,1)S(1)}, u32[]{:S(2)}, u32[]{:S(2)}) collective-permute-start(bf16[128,1536]{1,0:T(8,128)(2,1)S(1)} %get-tuple-element.17), channel_id=1, source_target_pairs={{0,8},{1,9},{2,10},{3,11},{4,12},{5,13},{6,14},{7,15},{8,0},{9,1},... | collective-permute-start | bytes 1179656 | tf_op jit(solution)/shard_map/ppermute | solution.py:152
  48.6 3.0 %collective-permute-start.4 = (bf16[128,1536]{1,0:T(8,128)(2,1)S(1)}, bf16[128,1536]{1,0:T(8,128)(2,1)S(1)}, u32[]{:S(2)}, u32[]{:S(2)}) collective-permute-start(bf16[128,1536]{1,0:T(8,128)(2,1)S(1)} %get-tuple-element.18), channel_id=1, source_target_pairs={{0,12},{1,13},{2,14},{3,15},{4,0},{5,1},{6,2},{7,3},{8,4},{9,5},{1... | collective-permute-start | bytes 1179656 | tf_op jit(solution)/shard_map/ppermute | solution.py:152
  51.6 3.0 %collective-permute-done.2.refs_5_.refs_1_ = bf16[128,1536]{1,0:T(8,128)(2,1)S(1)} collective-permute-done((bf16[128,1536]{1,0:T(8,128)(2,1)S(1)}, bf16[128,1536]{1,0:T(8,128)(2,1)S(1)}, u32[]{:S(2)}, u32[]{:S(2)}) %collective-permute-start.2) | collective-permute-done | bytes 393248 | tf_op jit(solution)/shard_map/ppermute | solution.py:152
  54.7 9.4 %collective-permute-done.3.refs_6_.refs_2_ = bf16[128,1536]{1,0:T(8,128)(2,1)S(1)} collective-permute-done((bf16[128,1536]{1,0:T(8,128)(2,1)S(1)}, bf16[128,1536]{1,0:T(8,128)(2,1)S(1)}, u32[]{:S(2)}, u32[]{:S(2)}) %collective-permute-start.3) | collective-permute-done | bytes 393248 | tf_op jit(solution)/shard_map/ppermute | solution.py:152
  64.1 1.1 %collective-permute-done.4.refs_7_.refs_3_ = bf16[128,1536]{1,0:T(8,128)(2,1)S(1)} collective-permute-done((bf16[128,1536]{1,0:T(8,128)(2,1)S(1)}, bf16[128,1536]{1,0:T(8,128)(2,1)S(1)}, u32[]{:S(2)}, u32[]{:S(2)}) %collective-permute-start.4) | collective-permute-done | bytes 393248 | tf_op jit(solution)/shard_map/ppermute | solution.py:152
  65.9 3.3 %collective-permute-start.8 = (bf16[512,512]{1,0:T(8,128)(2,1)S(1)}, bf16[512,512]{1,0:T(8,128)(2,1)}, u32[]{:S(2)}, u32[]{:S(2)}) collective-permute-start(bf16[512,512]{1,0:T(8,128)(2,1)S(1)} %get-tuple-element.24), channel_id=1, source_target_pairs={{0,1},{1,0},{2,3},{3,2},{4,5},{5,4},{6,7},{7,6},{8,9},{9,8},{10,11... | collective-permute-start | bytes 1572872 | tf_op jit(solution)/shard_map/ppermute | solution.py:204
  69.2 1.9 %shard_map.129 = (bf16[128,1024]{1,0:T(8,128)(2,1)S(1)}, bf16[128,1024]{1,0:T(8,128)(2,1)}, bf16[128,1024]{1,0:T(8,128)(2,1)S(1)}, bf16[128,1024]{1,0:T(8,128)(2,1)S(1)}) custom-call(s32[3]{0:T(128)S(1)} %pad_add_fusion.info.refs_0_, bf16[256,512]{1,0:T(8,128)(2,1)S(1)} %convert_bitcast_fusion.refs_1_, bf16[256,512]{1,0:T(8,128)(2,1)S(1)} %collective-permute-done.refs_2_, ...), custom_call_target="tpu_custom_call" | custom-call | flops 536870912 | bytes 4194304 | tf_op jit(solution)/shard_map/pallas_call | solution.py:94
  71.1 4.2 %collective-permute-start.5 = (bf16[128,1024]{1,0:T(8,128)(2,1)}, bf16[128,1024]{1,0:T(8,128)(2,1)S(1)}, u32[]{:S(2)}, u32[]{:S(2)}) collective-permute-start(bf16[128,1024]{1,0:T(8,128)(2,1)} %get-tuple-element.20), channel_id=1, source_target_pairs={{0,12},{1,13},{2,14},{3,15},{4,0},{5,1},{6,2},{7,3},{8,4},{9,5},{1... | collective-permute-start | bytes 786440 | tf_op jit(solution)/shard_map/ppermute | solution.py:192
  75.4 3.5 %collective-permute-start.6 = (bf16[128,1024]{1,0:T(8,128)(2,1)S(1)}, bf16[128,1024]{1,0:T(8,128)(2,1)S(1)}, u32[]{:S(2)}, u32[]{:S(2)}) collective-permute-start(bf16[128,1024]{1,0:T(8,128)(2,1)S(1)} %get-tuple-element.21), channel_id=1, source_target_pairs={{0,8},{1,9},{2,10},{3,11},{4,12},{5,13},{6,14},{7,15},{8,0},{9,1},... | collective-permute-start | bytes 786440 | tf_op jit(solution)/shard_map/ppermute | solution.py:192
  78.9 1.9 %collective-permute-start.7 = (bf16[128,1024]{1,0:T(8,128)(2,1)S(1)}, bf16[128,1024]{1,0:T(8,128)(2,1)S(1)}, u32[]{:S(2)}, u32[]{:S(2)}) collective-permute-start(bf16[128,1024]{1,0:T(8,128)(2,1)S(1)} %get-tuple-element.22), channel_id=1, source_target_pairs={{0,4},{1,5},{2,6},{3,7},{4,8},{5,9},{6,10},{7,11},{8,12},{9,13},{1... | collective-permute-start | bytes 786440 | tf_op jit(solution)/shard_map/ppermute | solution.py:192
  83.4 6.0 %all-to-all-start.2 = ((bf16[8,32,512]{2,1,0:T(8,128)(2,1)}), bf16[8,32,512]{2,1,0:T(8,128)(2,1)S(1)}, u32[]{:S(2)}, u32[]{:S(2)}) async-start(bf16[8,32,512]{2,1,0:T(8,128)(2,1)} %broadcast_in_dim.27), calls=%async_computation.2 | async-start | bytes 524288 | tf_op jit(solution)/shard_map/all_to_all | solution.py:193
  89.4 1.2 %convert_add_fusion = f32[512,512]{1,0:T(8,128)S(1)} fusion(f32[512,512]{1,0:T(8,128)S(1)} %get-tuple-element.23, bf16[512,512]{1,0:T(8,128)(2,1)} %collective-permute-done.8), kind=kLoop, calls=%fused_computation | loop fusion | flops 524288 | bytes 2621440 | tf_op jit(solution)/shard_map/add | solution.py:204
  90.6 1.0 copy-done.3
  91.7 2.1 %collective-permute-start.9 = (bf16[256,512]{1,0:T(8,128)(2,1)S(1)}, bf16[256,512]{1,0:T(8,128)(2,1)S(1)}, u32[]{:S(2)}, u32[]{:S(2)}) collective-permute-start(bf16[256,512]{1,0:T(8,128)(2,1)S(1)} %slice.45), channel_id=1, source_target_pairs={{0,2},{1,3},{2,0},{3,1},{4,6},{5,7},{6,4},{7,5},{8,10},{9,11},{10,... | collective-permute-start | bytes 786440 | tf_op jit(solution)/shard_map/ppermute | solution.py:205
  93.9 1.6 %shard_map.130 = bf16[128,4096]{1,0:T(8,128)(2,1)} custom-call(s32[3]{0:T(128)S(1)} %pad_add_fusion.info.refs_0_, bf16[128,1024]{1,0:T(8,128)(2,1)S(1)} %get-tuple-element.19.refs_0_, bf16[128,1024]{1,0:T(8,128)(2,1)S(1)} %collective-permute-done.5.refs_1_, bf16[128,1024]{1,0:T(8,128)(2,1)S(1)} %collective-permute-done.6.refs_2_, ...), custom_call_target="tpu_custom_call" | custom-call | bytes 2097152 | tf_op jit(solution)/shard_map/pallas_call | solution.py:94
  95.5 6.2 %collective-permute-done.9 = bf16[256,512]{1,0:T(8,128)(2,1)S(1)} collective-permute-done((bf16[256,512]{1,0:T(8,128)(2,1)S(1)}, bf16[256,512]{1,0:T(8,128)(2,1)S(1)}, u32[]{:S(2)}, u32[]{:S(2)}) %collective-permute-start.9) | collective-permute-done | bytes 262176 | tf_op jit(solution)/shard_map/ppermute | solution.py:205
  101.7 1.2 %fusion.4 = f32[1,256,512]{2,1,0:T(8,128)} fusion(f32[1,256,512]{2,1,0:T(8,128)S(1)} %copy-done.7, f32[512,512]{1,0:T(8,128)S(1)} %copy-done.4, bf16[256,512]{1,0:T(8,128)(2,1)S(1)} %collective-permute-done.9, f32[1,256,512]{2,1,0:T(8,128)S(1)} %copy-done.8, f32[1,256,512]{2,1,0:T(8,128)S(1)} %copy-done.6), kind=kLoop, calls=%fused_computation.9 | loop fusion | flops 1966080 | bytes 2883584 | tf_op jit(solution)/shard_map/broadcast_in_dim | solution.py:219
  (47 shorter events, 9.1 us)
Async XLA Ops:
  0.6 13.1 %copy-start = (s32[1,16]{1,0:T(1,128)S(1)}, s32[1,16]{1,0:T(1,128)}, u32[]{:S(2)}) copy-start(s32[1,16]{1,0:T(1,128)} %param.14) | copy-start | bytes 196
  1.7 9.7 %copy-start.5 = (f32[1,256,512]{2,1,0:T(8,128)S(1)}, f32[1,256,512]{2,1,0:T(8,128)}, u32[]{:S(2)}) copy-start(f32[1,256,512]{2,1,0:T(8,128)} %param.11) | copy-start | bytes 1572868
  2.5 24.1 %all-to-all-start = ((bf16[8,32,512]{2,1,0:T(8,128)(2,1)}), bf16[8,32,512]{2,1,0:T(8,128)(2,1)S(1)}, u32[]{:S(2)}, u32[]{:S(2)}) async-start(bf16[8,32,512]{2,1,0:T(8,128)(2,1)} %bitcast.13), calls=%async_computation | async-start | bytes 524288 | tf_op jit(solution)/shard_map/all_to_all | solution.py:132
  11.4 10.8 %collective-permute-start = (bf16[256,512]{1,0:T(8,128)(2,1)S(1)}, bf16[256,512]{1,0:T(8,128)(2,1)S(1)}, u32[]{:S(2)}, u32[]{:S(2)}) collective-permute-start(bf16[256,512]{1,0:T(8,128)(2,1)S(1)} %convert_bitcast_fusion.refs_1_), channel_id=1, source_target_pairs={{0,2},{1,3},{2,0},{3,1},{4,6},{5,7},{6,4},{7,5},{8,10},{9,11},{10,... | collective-permute-start | bytes 786440 | tf_op jit(solution)/shard_map/ppermute | solution.py:135
  13.7 0.7 copy-start.9
  13.7 0.7 copy-start.10
  14.4 25.8 %copy-start.1 = (bf16[1,128,4096]{2,1,0:T(8,128)(2,1)S(1)}, bf16[1,128,4096]{2,1,0:T(8,128)(2,1)}, u32[]{:S(2)}) copy-start(bf16[1,128,4096]{2,1,0:T(8,128)(2,1)} %param.9) | copy-start | bytes 3145732
  23.0 46.2 %collective-permute-start.1 = (bf16[512,512]{1,0:T(8,128)(2,1)}, bf16[512,512]{1,0:T(8,128)(2,1)S(1)}, u32[]{:S(2)}, u32[]{:S(2)}) collective-permute-start(bf16[512,512]{1,0:T(8,128)(2,1)} %pad_maximum_fusion), channel_id=1, source_target_pairs={{0,1},{1,0},{2,3},{3,2},{4,5},{5,4},{6,7},{7,6},{8,9},{9,8},{10,11... | collective-permute-start | bytes 1572872 | tf_op jit(solution)/shard_map/ppermute | solution.py:136
  27.3 12.9 %copy-start.2 = (bf16[1,128,512]{2,1,0:T(8,128)(2,1)S(1)}, bf16[1,128,512]{2,1,0:T(8,128)(2,1)}, u32[]{:S(2)}) copy-start(bf16[1,128,512]{2,1,0:T(8,128)(2,1)} %param.10) | copy-start | bytes 393220
  27.3 53.6 %all-to-all-start.1 = ((bf16[4,48,512]{2,1,0:T(8,128)(2,1)}), bf16[4,48,512]{2,1,0:T(8,128)(2,1)}, u32[]{:S(2)}, u32[]{:S(2)}) async-start(bf16[4,48,512]{2,1,0:T(8,128)(2,1)} %broadcast_in_dim.26), calls=%async_computation.1 | async-start | bytes 393216 | tf_op jit(solution)/shard_map/all_to_all | solution.py:162
  40.9 13.8 %collective-permute-start.2 = (bf16[128,1536]{1,0:T(8,128)(2,1)S(1)}, bf16[128,1536]{1,0:T(8,128)(2,1)S(1)}, u32[]{:S(2)}, u32[]{:S(2)}) collective-permute-start(bf16[128,1536]{1,0:T(8,128)(2,1)S(1)} %get-tuple-element.16), channel_id=1, source_target_pairs={{0,4},{1,5},{2,6},{3,7},{4,8},{5,9},{6,10},{7,11},{8,12},{9,13},{1... | collective-permute-start | bytes 1179656 | tf_op jit(solution)/shard_map/ppermute | solution.py:152
  44.1 20.0 %collective-permute-start.3 = (bf16[128,1536]{1,0:T(8,128)(2,1)S(1)}, bf16[128,1536]{1,0:T(8,128)(2,1)S(1)}, u32[]{:S(2)}, u32[]{:S(2)}) collective-permute-start(bf16[128,1536]{1,0:T(8,128)(2,1)S(1)} %get-tuple-element.17), channel_id=1, source_target_pairs={{0,8},{1,9},{2,10},{3,11},{4,12},{5,13},{6,14},{7,15},{8,0},{9,1},... | collective-permute-start | bytes 1179656 | tf_op jit(solution)/shard_map/ppermute | solution.py:152
  48.6 16.6 %collective-permute-start.4 = (bf16[128,1536]{1,0:T(8,128)(2,1)S(1)}, bf16[128,1536]{1,0:T(8,128)(2,1)S(1)}, u32[]{:S(2)}, u32[]{:S(2)}) collective-permute-start(bf16[128,1536]{1,0:T(8,128)(2,1)S(1)} %get-tuple-element.18), channel_id=1, source_target_pairs={{0,12},{1,13},{2,14},{3,15},{4,0},{5,1},{6,2},{7,3},{8,4},{9,5},{1... | collective-permute-start | bytes 1179656 | tf_op jit(solution)/shard_map/ppermute | solution.py:152
  65.9 23.5 %collective-permute-start.8 = (bf16[512,512]{1,0:T(8,128)(2,1)S(1)}, bf16[512,512]{1,0:T(8,128)(2,1)}, u32[]{:S(2)}, u32[]{:S(2)}) collective-permute-start(bf16[512,512]{1,0:T(8,128)(2,1)S(1)} %get-tuple-element.24), channel_id=1, source_target_pairs={{0,1},{1,0},{2,3},{3,2},{4,5},{5,4},{6,7},{7,6},{8,9},{9,8},{10,11... | collective-permute-start | bytes 1572872 | tf_op jit(solution)/shard_map/ppermute | solution.py:204
  71.1 22.6 %collective-permute-start.5 = (bf16[128,1024]{1,0:T(8,128)(2,1)}, bf16[128,1024]{1,0:T(8,128)(2,1)S(1)}, u32[]{:S(2)}, u32[]{:S(2)}) collective-permute-start(bf16[128,1024]{1,0:T(8,128)(2,1)} %get-tuple-element.20), channel_id=1, source_target_pairs={{0,12},{1,13},{2,14},{3,15},{4,0},{5,1},{6,2},{7,3},{8,4},{9,5},{1... | collective-permute-start | bytes 786440 | tf_op jit(solution)/shard_map/ppermute | solution.py:192
  75.4 18.4 %collective-permute-start.6 = (bf16[128,1024]{1,0:T(8,128)(2,1)S(1)}, bf16[128,1024]{1,0:T(8,128)(2,1)S(1)}, u32[]{:S(2)}, u32[]{:S(2)}) collective-permute-start(bf16[128,1024]{1,0:T(8,128)(2,1)S(1)} %get-tuple-element.21), channel_id=1, source_target_pairs={{0,8},{1,9},{2,10},{3,11},{4,12},{5,13},{6,14},{7,15},{8,0},{9,1},... | collective-permute-start | bytes 786440 | tf_op jit(solution)/shard_map/ppermute | solution.py:192
  78.9 14.9 %collective-permute-start.7 = (bf16[128,1024]{1,0:T(8,128)(2,1)S(1)}, bf16[128,1024]{1,0:T(8,128)(2,1)S(1)}, u32[]{:S(2)}, u32[]{:S(2)}) collective-permute-start(bf16[128,1024]{1,0:T(8,128)(2,1)S(1)} %get-tuple-element.22), channel_id=1, source_target_pairs={{0,4},{1,5},{2,6},{3,7},{4,8},{5,9},{6,10},{7,11},{8,12},{9,13},{1... | collective-permute-start | bytes 786440 | tf_op jit(solution)/shard_map/ppermute | solution.py:192
  83.4 20.1 %all-to-all-start.2 = ((bf16[8,32,512]{2,1,0:T(8,128)(2,1)}), bf16[8,32,512]{2,1,0:T(8,128)(2,1)S(1)}, u32[]{:S(2)}, u32[]{:S(2)}) async-start(bf16[8,32,512]{2,1,0:T(8,128)(2,1)} %broadcast_in_dim.27), calls=%async_computation.2 | async-start | bytes 524288 | tf_op jit(solution)/shard_map/all_to_all | solution.py:193
  90.6 1.0 copy-start.3
  91.6 10.0 %copy-start.8 = (f32[1,256,512]{2,1,0:T(8,128)S(1)}, f32[1,256,512]{2,1,0:T(8,128)}, u32[]{:S(2)}) copy-start(f32[1,256,512]{2,1,0:T(8,128)} %param.12) | copy-start | bytes 1572868
  91.7 10.0 %collective-permute-start.9 = (bf16[256,512]{1,0:T(8,128)(2,1)S(1)}, bf16[256,512]{1,0:T(8,128)(2,1)S(1)}, u32[]{:S(2)}, u32[]{:S(2)}) collective-permute-start(bf16[256,512]{1,0:T(8,128)(2,1)S(1)} %slice.45), channel_id=1, source_target_pairs={{0,2},{1,3},{2,0},{3,1},{4,6},{5,7},{6,4},{7,5},{8,10},{9,11},{10,... | collective-permute-start | bytes 786440 | tf_op jit(solution)/shard_map/ppermute | solution.py:205
  93.8 7.9 %copy-start.4 = (f32[512,512]{1,0:T(8,128)S(1)}, f32[512,512]{1,0:T(8,128)}, u32[]{:S(2)}) copy-start(f32[512,512]{1,0:T(8,128)} %copy-done.3) | copy-start | bytes 3145732
  93.8 7.9 %copy-start.6 = (f32[1,256,512]{2,1,0:T(8,128)S(1)}, f32[1,256,512]{2,1,0:T(8,128)}, u32[]{:S(2)}) copy-start(f32[1,256,512]{2,1,0:T(8,128)} %param.11) | copy-start | bytes 1572868
  93.8 7.8 %copy-start.7 = (f32[1,256,512]{2,1,0:T(8,128)S(1)}, f32[1,256,512]{2,1,0:T(8,128)}, u32[]{:S(2)}) copy-start(f32[1,256,512]{2,1,0:T(8,128)} %param.13) | copy-start | bytes 1572868

commit v3 on v1

v3 whole, which is shorter than its diff:
```python
import math

import jax
import jax.numpy as jnp
from jax import lax
from jax.experimental import pallas as pl
from jax.experimental.pallas import tpu as pltpu
from jax.sharding import PartitionSpec as P

QUAD = 4
COLUMN = 4
SIDES = 2
NEAR = SIDES * QUAD
NEAR_ORDER = ((0, 1), (0, 2), (0, 0), (0, 3), (1, 1), (1, 2), (1, 0), (1, 3))
FAR_ORDER = (2, 3, 1, 0)
HALF = jnp.bfloat16
FULL = jnp.float32
SMEM = pl.BlockSpec(memory_space=pltpu.SMEM)
VMEM = pl.BlockSpec(memory_space=pltpu.VMEM)
ANY = pl.BlockSpec(memory_space=pl.ANY)


def block_of(place, step):
    return place ^ (((step & 1) << 1) | (step >> 1))


def split_kernel(whole, pieces):
    share = pieces.shape[1] // COLUMN
    far = pieces.shape[1] // share
    for i, (h, b) in enumerate(NEAR_ORDER):
        starts = [((h * far + a) * QUAD + b) * share for a in range(far)]
        rows = [whole[start : start + share] for start in starts]
        pieces[i] = jnp.concatenate(rows, axis=0).astype(HALF)


def join_kernel(pieces, whole):
    share = pieces.shape[1] // COLUMN
    far = pieces.shape[1] // share
    parts = {key: pieces[i].astype(FULL) for i, key in enumerate(NEAR_ORDER)}
    for h in range(SIDES):
        for a in range(far):
            rows = [parts[h, b][a * share : (a + 1) * share] for b in range(QUAD)]
            start = (h * far + a) * QUAD * share
            whole[start : start + QUAD * share] = jnp.concatenate(rows, axis=0).astype(HALF)


def pack_kernel(lengths, features, cotangent, after, *packed):
    me = lax.axis_index("fsdp")
    place, y = me % QUAD, me // QUAD
    block = features.shape[1] // (COLUMN * QUAD)
    row = lax.broadcasted_iota(jnp.int32, cotangent.shape, 0)
    masked = jnp.where(row < lengths[0, me], cotangent[...], jnp.zeros((), cotangent.dtype))
    for d in range(COLUMN):
        target = (y + d) % COLUMN
        for step in range(QUAD):
            source = pl.multiple_of((target * QUAD + block_of(place, step)) * block, block)
            packed[d][:, step * block : (step + 1) * block] = features[:, pl.ds(source, block)]
        packed[d][:, QUAD * block :] = masked


def sum_kernel(pieces, anchor, momentum, after, sums):
    total = pieces[0].astype(FULL)
    for i in range(1, NEAR):
        total += pieces[i].astype(FULL)
    base = anchor[...] - 0.7 * 0.9 * 0.9 * momentum[...]
    high = base.astype(HALF).astype(FULL)
    value = jnp.concatenate([total, high, base - high], axis=0).astype(HALF)
    for i in range(sums.shape[0]):
        sums[i] = value


def update_kernel(sums, anchor, momentum, anchor_out, momentum_out, fresh, delta):
    share = anchor.shape[0]
    far = sums.shape[0]
    near_rows = far * share
    parts = [sums[i].astype(FULL) for i in range(far)]
    total = parts[0][:near_rows]
    for part in parts[1:]:
        total += part[:near_rows]
    total = total / (NEAR * far)
    delta[...] = total
    place = lax.axis_index("replica") // QUAD % far
    own = delta[pl.ds(pl.multiple_of(place * share, share), share), :]
    moved = 0.9 * momentum[...] + own
    momentum_out[...] = moved
    anchor_out[...] = anchor[...] - 0.7 * (own + 0.9 * moved)
    parts = [parts[FAR_ORDER.index(a)][near_rows:] for a in range(far)]
    bases = [part[:share] + part[share:] for part in parts]
    value = (jnp.concatenate(bases, axis=0) - 0.7 * 1.9 * total).astype(HALF)
    for i in range(NEAR):
        fresh[i] = value


def input_kernel(factor, after, own, beside, across, *refs):
    cotangents, results = refs[:COLUMN], refs[COLUMN:]
    tokens = cotangents[0].shape[0]
    block = own.shape[0]
    left = jnp.concatenate([ref[...] for ref in cotangents], axis=0)
    for step, right in enumerate((own[...], beside[...], across[:block], across[block:])):
        product = lax.dot_general(left, right, (((1,), (1,)), ((), ())), preferred_element_type=FULL)
        product = (product * factor).astype(HALF)
        for d in range(COLUMN):
            results[d][:, step * block : (step + 1) * block] = product[d * tokens : (d + 1) * tokens]


def weight_kernel(*refs):
    packed, (after, own, passed, sent) = refs[:COLUMN], refs[COLUMN:]
    rows, keys = own.shape

    def columns(start, size):
        return jnp.concatenate([ref[:, start : start + size] for ref in packed], axis=0)

    def term(start, size):
        return lax.dot_general(
            columns(start, size), right, (((0,), (0,)), ((), ())), preferred_element_type=FULL
        )

    right = columns(QUAD * rows, keys)
    sent[...] = term(2 * rows, 2 * rows).astype(HALF)
    own[...] = term(0, rows)
    passed[...] = term(rows, rows)


def unpack_kernel(*refs):
    pieces, result, done = refs[:COLUMN], refs[COLUMN], refs[COLUMN + 1]
    me = lax.axis_index("fsdp")
    place, y = me % QUAD, me // QUAD
    block = result.shape[1] // (COLUMN * QUAD)
    copies = []
    for d in range(COLUMN):
        for step in range(QUAD):
            target = ((y + d) % COLUMN * QUAD + block_of(place, step)) * block
            copies.append(
                pltpu.make_async_copy(
                    pieces[d].at[:, pl.ds(step * block, block)],
                    result.at[:, pl.ds(pl.multiple_of(target, block), block)],
                    done.at[d * QUAD + step],
                )
            )
    for copy in copies:
        copy.start()
    for copy in copies:
        copy.wait()


def whole(shape):
    return pl.BlockSpec(shape, lambda *_: (0,) * len(shape))


def call(kernel, outs, ins, in_specs=None, out_specs=None, flops=0, moved=1 << 20, scratch=(), grid=()):
    outs = [jax.ShapeDtypeStruct(shape, dtype) for shape, dtype in outs]
    return pl.pallas_call(
        kernel,
        grid=grid,
        out_shape=outs,
        in_specs=in_specs or [VMEM] * len(ins),
        out_specs=out_specs or [whole(out.shape) for out in outs],
        scratch_shapes=scratch,
        compiler_params=pltpu.CompilerParams(vmem_limit_bytes=48 << 20),
        cost_estimate=pl.CostEstimate(flops=flops, bytes_accessed=moved, transcendentals=0),
    )(*ins)


def local(
    activations, cotangent, master, moment_one, moment_two, lengths, pseudo_grad, anchor, momentum
):
    shards = lax.axis_size("fsdp")
    replicas = lax.axis_size("replica")
    tokens, width = activations.shape[1:]
    keys = cotangent.shape[2]
    share = anchor.shape[1]
    rows = master.shape[1]
    wide = width // COLUMN
    factor = 1.0 / math.sqrt(width)
    flops = 2 * COLUMN * tokens * wide * keys

    beside = [(f, f ^ 2) for f in range(shards)]
    across = [(f, f ^ 1) for f in range(shards)]
    up = [[(f, (f + QUAD * d) % shards) for f in range(shards)] for d in range(COLUMN)]
    down = [[(f, (f - QUAD * d) % shards) for f in range(shards)] for d in range(COLUMN)]
    depth = replicas // SIDES
    outer = depth // QUAD
    near = [[depth * h + QUAD * a + b for h, b in NEAR_ORDER] for a in range(outer)]
    far = [[depth * h + QUAD * a + b for a in FAR_ORDER] for h in range(SIDES) for b in range(QUAD)]

    (pieces,) = call(split_kernel, [((NEAR, outer * share, keys), HALF)], (pseudo_grad[0, 0],))
    near_pieces = lax.all_to_all(pieces, "replica", 0, 0, axis_index_groups=near)

    packed = call(
        pack_kernel,
        [((tokens, wide + keys), HALF)] * COLUMN,
        (lengths, activations[0], cotangent[0], pieces),
        [SMEM, VMEM, VMEM, ANY],
        moved=3 << 20,
    )
    packed = [packed[0]] + [lax.ppermute(packed[d], "fsdp", up[d]) for d in (1, 2, 3)]

    raw = lax.optimization_barrier((master[0], packed[0]))[0]
    own = raw.astype(HALF)
    other = lax.ppermute(own, "fsdp", beside)

    (sums,) = call(
        sum_kernel,
        [((outer, (outer + 2) * share, keys), HALF)],
        (near_pieces, anchor[0], momentum[0], packed[0]),
        [VMEM, VMEM, VMEM, ANY],
    )
    other = lax.optimization_barrier((other, sums, packed[1], packed[2], packed[3]))[0]
    both = lax.ppermute(jnp.concatenate([own, other], axis=0), "fsdp", across)
    sums = lax.all_to_all(sums, "replica", 0, 0, axis_index_groups=far)
    anchor_out, momentum_out, fresh = call(
        update_kernel,
        [((share, keys), FULL), ((share, keys), FULL), ((NEAR, outer * share, keys), HALF)],
        (sums, anchor[0], momentum[0]),
        scratch=[pltpu.VMEM((outer * share, keys), FULL)],
    )
    spread = lax.all_to_all(fresh, "replica", 0, 0, axis_index_groups=near)
    (spread,) = call(join_kernel, [(pseudo_grad.shape[2:], HALF)], (spread,))

    cot_spec = pl.BlockSpec((tokens, keys), lambda *_: (0, wide // keys))
    products = call(
        lambda *refs: input_kernel(factor, *refs),
        [((tokens, wide), HALF)] * COLUMN,
        (fresh, own, other, both, *packed),
        [ANY, whole(own.shape), whole(own.shape), whole(both.shape)] + [cot_spec] * COLUMN,
        flops=flops,
        moved=3 << 20,
        grid=(1,),
    )
    back = [products[0]] + [lax.ppermute(products[d], "fsdp", down[d]) for d in (1, 2, 3)]

    grad_own, grad_passed, sent = call(
        weight_kernel,
        [((rows, keys), FULL), ((rows, keys), FULL), ((2 * rows, keys), HALF)],
        (*packed, products[0]),
        [VMEM] * COLUMN + [ANY],
        flops=flops,
        moved=5 << 20,
    )
    crossed = lax.ppermute(sent, "fsdp", across).astype(FULL)
    passed = lax.ppermute((grad_passed + crossed[rows:]).astype(HALF), "fsdp", beside)
    summed = grad_own + crossed[:rows] + passed.astype(FULL)

    grad = summed * factor
    first = 0.9 * moment_one[0] + 0.1 * grad
    second = 0.95 * moment_two[0] + 0.05 * grad * grad
    master_out = master[0] * (1.0 - 0.1 * 0.1) - 0.1 * first / (jnp.sqrt(second) + 1e-08)

    (input_grad,) = call(
        unpack_kernel,
        [((tokens, width), HALF)],
        back,
        [ANY] * COLUMN,
        [ANY],
        scratch=[pltpu.SemaphoreType.DMA((COLUMN * QUAD,))],
        moved=2 << 20,
    )
    return (
        input_grad[None], master_out[None], spread[None], anchor_out[None], momentum_out[None]
    )


def solution(mesh):
    placed = (
        P("replica", "fsdp", None),
        P("replica", "fsdp", None),
        P("replica", "fsdp", None),
        P("replica", "fsdp", None),
        P("replica", "fsdp", None),
        P("replica", None),
        P("replica", "fsdp", None, None),
        P("fsdp", "replica", None),
        P("fsdp", "replica", None),
    )
    return jax.shard_map(
        local,
        mesh=mesh,
        in_specs=placed,
        out_specs=(
            P("replica", "fsdp", None),
            P("replica", "fsdp", None),
            P("fsdp", None, None),
            P("fsdp", "replica", None),
            P("fsdp", "replica", None),
        ),
        check_vma=False,
    )
```

time: 127 us -> 87.4 us (0.69)
  waiting for transfers between devices: 59.7 us -> 10.5 us
  starting transfers between devices: 30.6 us -> 63.5 us
  between operations: 14.2 us -> 0.94 us
  Pallas kernels: 0 us -> 7.73 us
  matrix products: 7.4 us -> 0 us
  local copies, waits for them, and re-layouts: 8.46 us -> 2.5 us
  other arithmetic: 6.52 us -> 1.5 us
    all_to_all x3, waiting for transfers between devices: 53.3 us -> 2.13 us  [the longest x1 2.13 us: local(): sums = lax.all_to_all(sums, 'replica', 0, 0, axis_index_groups=far)]
    ppermute x0 -> x10, starting transfers between devices: none -> 32.6 us  [the longest x3 10.7 us: local(): lax.ppermute(packed[d], 'fsdp', up[d])]
    ppermute x0 -> x10, waiting for transfers between devices: none -> 8.36 us  [the longest x3 8.34 us: local(): lax.ppermute(products[d], 'fsdp', down[d])]
    pallas_call x0 -> x8, Pallas kernels: none -> 7.73 us  [call(): pl.pallas_call(kernel, grid=grid, out_shape=outs, in_specs=in_specs or [V...]
    dot_general x2 -> x0, matrix products: 7.4 us -> none  [the longest x1 4.65 us: local(): lax.dot_general(masked, weights, (((1,), (1,)), ((), ())), preferred_elem...]
    all_gather x2 -> x0, waiting for transfers between devices: 6.4 us -> none  [the longest x1 6.4 us: local(): lax.all_gather(master[0].astype(jnp.bfloat16), 'fsdp', axis=0, tiled=True)]
    unnamed x26 -> x28, local copies, waits for them, and re-layouts: 6.63 us -> 2.5 us
    convert_element_type x2 -> x3, other arithmetic: 3.56 us -> 0.25 us  [the longest x1 0.12 us: local(): crossed = lax.ppermute(sent, 'fsdp', across).astype(FULL)]
  transfers between devices with their start and end apart: 5 -> 13, of which waited for: 4 -> 3; matrix products, arithmetic and copies ran while one was open for 11% -> 2% of each run, Pallas kernels for 0% -> 5%
where the time goes in v3:
time: 87.4 us; the launch traced here: 86.6 us
  starting transfers between devices  63.5 us (73%)
  waiting for transfers between devices  10.5 us (12%)
  Pallas kernels  7.73 us (9%)
  local copies, waits for them, and re-layouts  2.5 us (3%)
  other arithmetic  1.5 us (2%)
  between operations  0.94 us (1%)
    all_to_all x1, starting transfers between devices, local(): sums = lax.all_to_all(sums, 'replica', 0, 0, axis_index_groups=far)  14.2 us
    ppermute x3, starting transfers between devices, local(): lax.ppermute(packed[d], 'fsdp', up[d])  10.7 us
    all_to_all x1, starting transfers between devices, local(): lax.all_to_all(pieces, 'replica', 0, 0, axis_index_groups=near)  9.32 us
    ppermute x3, waiting for transfers between devices, local(): lax.ppermute(products[d], 'fsdp', down[d])  8.34 us
    ppermute x3, starting transfers between devices, local(): lax.ppermute(products[d], 'fsdp', down[d])  7.92 us
    pallas_call x8, Pallas kernels, call(): pl.pallas_call(kernel, grid=grid, out_shape=outs, in_specs=in_specs or [V...  7.73 us
    all_to_all x1, starting transfers between devices, local(): spread = lax.all_to_all(fresh, 'replica', 0, 0, axis_index_groups=near)  7.28 us
    ppermute x1, starting transfers between devices, local(): crossed = lax.ppermute(sent, 'fsdp', across).astype(FULL)  4.93 us
  transfers between devices with their start and end apart: 13, of which 3 were waited for; matrix products, arithmetic and copies ran while one was open for 2% of the time, Pallas kernels for 5%

profile of v3, /device:TPU:1, one launch (start us, length us, event | category | flops | bytes accessed | tf_op | source)
XLA Modules:
  0.0 86.6 jit_solution(3477438376617698383)
XLA Ops:
  0.7 1.1 %copy-done.1 = f32[1,1,256,512]{3,2,1,0:T(8,128)S(1)} copy-done((f32[1,1,256,512]{3,2,1,0:T(8,128)S(1)}, f32[1,1,256,512]{3,2,1,0:T(8,128)}, u32[]{:S(2)}) %copy-start.1) | copy-done | bytes 524312
  1.8 0.7 shard_map.128.after
  2.5 9.3 %all-to-all-start = ((bf16[8,32,512]{2,1,0:T(8,128)(2,1)}), bf16[8,32,512]{2,1,0:T(8,128)(2,1)S(1)}, u32[]{:S(2)}, u32[]{:S(2)}) async-start(bf16[8,32,512]{2,1,0:T(8,128)(2,1)} %shard_map.128.after), calls=%async_computation | async-start | bytes 524288 | tf_op jit(solution)/shard_map/all_to_all | solution.py:187
  12.5 1.6 %shard_map.129 = (bf16[128,1536]{1,0:T(8,128)(2,1)S(1)}, bf16[128,1536]{1,0:T(8,128)(2,1)}, bf16[128,1536]{1,0:T(8,128)(2,1)}, bf16[128,1536]{1,0:T(8,128)(2,1)S(1)}) custom-call(s32[1,16]{1,0:T(1,128)S(1)} %copy-done.5, bf16[128,4096]{1,0:T(8,128)(2,1)S(1)} %bitcast.31, bf16[128,512]{1,0:T(8,128)(2,1)S(1)} %bitcast.33, bf16[8,32,512]{2,1,0:T(8,128)(2,1)} %shard_map.128.after), custom_call_target="tpu_custom_call" | custom-call | bytes 3145728 | tf_op jit(solution)/shard_map/pallas_call | solution.py:152
  14.1 3.2 %collective-permute-start.1 = (bf16[128,1536]{1,0:T(8,128)(2,1)}, bf16[128,1536]{1,0:T(8,128)(2,1)S(1)}, u32[]{:S(2)}, u32[]{:S(2)}) collective-permute-start(bf16[128,1536]{1,0:T(8,128)(2,1)} %get-tuple-element.24), channel_id=1, source_target_pairs={{0,4},{1,5},{2,6},{3,7},{4,8},{5,9},{6,10},{7,11},{8,12},{9,13},{1... | collective-permute-start | bytes 1179656 | tf_op jit(solution)/shard_map/ppermute | solution.py:196
  17.3 4.5 %collective-permute-start.2 = (bf16[128,1536]{1,0:T(8,128)(2,1)}, bf16[128,1536]{1,0:T(8,128)(2,1)S(1)}, u32[]{:S(2)}, u32[]{:S(2)}) collective-permute-start(bf16[128,1536]{1,0:T(8,128)(2,1)} %get-tuple-element.25), channel_id=1, source_target_pairs={{0,8},{1,9},{2,10},{3,11},{4,12},{5,13},{6,14},{7,15},{8,0},{9,1},... | collective-permute-start | bytes 1179656 | tf_op jit(solution)/shard_map/ppermute | solution.py:196
  21.8 3.0 %collective-permute-start.3 = (bf16[128,1536]{1,0:T(8,128)(2,1)S(1)}, bf16[128,1536]{1,0:T(8,128)(2,1)S(1)}, u32[]{:S(2)}, u32[]{:S(2)}) collective-permute-start(bf16[128,1536]{1,0:T(8,128)(2,1)S(1)} %get-tuple-element.26), channel_id=1, source_target_pairs={{0,12},{1,13},{2,14},{3,15},{4,0},{5,1},{6,2},{7,3},{8,4},{9,5},{1... | collective-permute-start | bytes 1179656 | tf_op jit(solution)/shard_map/ppermute | solution.py:196
  24.9 2.2 %collective-permute-start = (bf16[256,512]{1,0:T(8,128)(2,1)S(1)}, bf16[256,512]{1,0:T(8,128)(2,1)S(1)}, u32[]{:S(2)}, u32[]{:S(2)}) collective-permute-start(bf16[256,512]{1,0:T(8,128)(2,1)S(1)} %convert_element_type.12.refs_1_), channel_id=1, source_target_pairs={{0,2},{1,3},{2,0},{3,1},{4,6},{5,7},{6,4},{7,5},{8,10},{9,11},{10,... | collective-permute-start | bytes 786440 | tf_op jit(solution)/shard_map/ppermute | solution.py:200
  27.8 14.2 %all-to-all-start.1 = ((bf16[4,48,512]{2,1,0:T(8,128)(2,1)}), bf16[4,48,512]{2,1,0:T(8,128)(2,1)S(1)}, u32[]{:S(2)}, u32[]{:S(2)}) async-start(bf16[4,48,512]{2,1,0:T(8,128)(2,1)} %shard_map.130), calls=%async_computation.1 | async-start | bytes 393216 | tf_op jit(solution)/shard_map/all_to_all | solution.py:210
  42.1 4.8 %collective-permute-start.4 = (bf16[512,512]{1,0:T(8,128)(2,1)S(1)}, bf16[512,512]{1,0:T(8,128)(2,1)S(1)}, u32[]{:S(2)}, u32[]{:S(2)}) collective-permute-start(bf16[512,512]{1,0:T(8,128)(2,1)S(1)} %pad_maximum_fusion), channel_id=1, source_target_pairs={{0,1},{1,0},{2,3},{3,2},{4,5},{5,4},{6,7},{7,6},{8,9},{9,8},{10,11... | collective-permute-start | bytes 1572872 | tf_op jit(solution)/shard_map/ppermute | solution.py:209
  46.9 2.1 %all-to-all-done.1.sums = bf16[4,48,512]{2,1,0:T(8,128)(2,1)S(1)} async-done(((bf16[4,48,512]{2,1,0:T(8,128)(2,1)}), bf16[4,48,512]{2,1,0:T(8,128)(2,1)S(1)}, u32[]{:S(2)}, u32[]{:S(2)}) %all-to-all-start.1) | async-done | bytes 196640 | tf_op jit(solution)/shard_map/all_to_all | solution.py:210
  49.1 0.8 shard_map.131
  49.8 0.7 shard_map.132
  51.3 1.4 %shard_map.134 = (f32[256,512]{1,0:T(8,128)S(1)}, f32[256,512]{1,0:T(8,128)S(1)}, bf16[512,512]{1,0:T(8,128)(2,1)}) custom-call(bf16[128,1536]{1,0:T(8,128)(2,1)S(1)} %get-tuple-element.21.after.refs_4_.refs_0_, bf16[128,1536]{1,0:T(8,128)(2,1)S(1)} %collective-permute-done.1.refs_5_.refs_1_, bf16[128,1536]{1,0:T(8,128)(2,1)S(1)} %collective-permute-done.2.refs_6_.refs_2_, ...), custom_call_target="tpu_custom_call" | custom-call | flops 536870912 | bytes 5242880 | tf_op jit(solution)/shard_map/pallas_call | solution.py:152
  52.7 4.9 %collective-permute-start.8 = (bf16[512,512]{1,0:T(8,128)(2,1)}, bf16[512,512]{1,0:T(8,128)(2,1)S(1)}, u32[]{:S(2)}, u32[]{:S(2)}) collective-permute-start(bf16[512,512]{1,0:T(8,128)(2,1)} %get-tuple-element.33), channel_id=1, source_target_pairs={{0,1},{1,0},{2,3},{3,2},{4,5},{5,4},{6,7},{7,6},{8,9},{9,8},{10,11... | collective-permute-start | bytes 1572872 | tf_op jit(solution)/shard_map/ppermute | solution.py:240
  57.6 7.3 %all-to-all-start.2 = ((bf16[8,32,512]{2,1,0:T(8,128)(2,1)}), bf16[8,32,512]{2,1,0:T(8,128)(2,1)S(1)}, u32[]{:S(2)}, u32[]{:S(2)}) async-start(bf16[8,32,512]{2,1,0:T(8,128)(2,1)} %get-tuple-element.22.refs_0_), calls=%async_computation.2 | async-start | bytes 524288 | tf_op jit(solution)/shard_map/all_to_all | solution.py:217
  64.9 1.9 %collective-permute-start.5 = (bf16[128,1024]{1,0:T(8,128)(2,1)S(1)}, bf16[128,1024]{1,0:T(8,128)(2,1)S(1)}, u32[]{:S(2)}, u32[]{:S(2)}) collective-permute-start(bf16[128,1024]{1,0:T(8,128)(2,1)S(1)} %copy-done.9), channel_id=1, source_target_pairs={{0,12},{1,13},{2,14},{3,15},{4,0},{5,1},{6,2},{7,3},{8,4},{9,5},{1... | collective-permute-start | bytes 786440 | tf_op jit(solution)/shard_map/ppermute | solution.py:230
  66.8 4.1 %collective-permute-start.6 = (bf16[128,1024]{1,0:T(8,128)(2,1)S(1)}, bf16[128,1024]{1,0:T(8,128)(2,1)S(1)}, u32[]{:S(2)}, u32[]{:S(2)}) collective-permute-start(bf16[128,1024]{1,0:T(8,128)(2,1)S(1)} %copy-done.7), channel_id=1, source_target_pairs={{0,8},{1,9},{2,10},{3,11},{4,12},{5,13},{6,14},{7,15},{8,0},{9,1},... | collective-permute-start | bytes 786440 | tf_op jit(solution)/shard_map/ppermute | solution.py:230
  70.9 1.9 %collective-permute-start.7 = (bf16[128,1024]{1,0:T(8,128)(2,1)S(1)}, bf16[128,1024]{1,0:T(8,128)(2,1)S(1)}, u32[]{:S(2)}, u32[]{:S(2)}) collective-permute-start(bf16[128,1024]{1,0:T(8,128)(2,1)S(1)} %get-tuple-element.31), channel_id=1, source_target_pairs={{0,4},{1,5},{2,6},{3,7},{4,8},{5,9},{6,10},{7,11},{8,12},{9,13},{1... | collective-permute-start | bytes 786440 | tf_op jit(solution)/shard_map/ppermute | solution.py:230
  73.1 2.1 %collective-permute-start.9 = (bf16[256,512]{1,0:T(8,128)(2,1)S(1)}, bf16[256,512]{1,0:T(8,128)(2,1)S(1)}, u32[]{:S(2)}, u32[]{:S(2)}) collective-permute-start(bf16[256,512]{1,0:T(8,128)(2,1)S(1)} %fusion), channel_id=1, source_target_pairs={{0,2},{1,3},{2,0},{3,1},{4,6},{5,7},{6,4},{7,5},{8,10},{9,11},{10,... | collective-permute-start | bytes 786440 | tf_op jit(solution)/shard_map/ppermute | solution.py:241
  75.2 2.0 %collective-permute-done.6.refs_2_ = bf16[128,1024]{1,0:T(8,128)(2,1)S(1)} collective-permute-done((bf16[128,1024]{1,0:T(8,128)(2,1)S(1)}, bf16[128,1024]{1,0:T(8,128)(2,1)S(1)}, u32[]{:S(2)}, u32[]{:S(2)}) %collective-permute-start.6) | collective-permute-done | bytes 262176 | tf_op jit(solution)/shard_map/ppermute | solution.py:230
  77.2 6.3 %collective-permute-done.7.refs_3_ = bf16[128,1024]{1,0:T(8,128)(2,1)S(1)} collective-permute-done((bf16[128,1024]{1,0:T(8,128)(2,1)S(1)}, bf16[128,1024]{1,0:T(8,128)(2,1)S(1)}, u32[]{:S(2)}, u32[]{:S(2)}) %collective-permute-start.7) | collective-permute-done | bytes 262176 | tf_op jit(solution)/shard_map/ppermute | solution.py:230
  83.5 1.1 %shard_map.133 = bf16[128,4096]{1,0:T(8,128)(2,1)} custom-call(bf16[128,1024]{1,0:T(8,128)(2,1)S(1)} %get-tuple-element.28.refs_0_.refs_4_, bf16[128,1024]{1,0:T(8,128)(2,1)S(1)} %collective-permute-done.5.refs_1_, bf16[128,1024]{1,0:T(8,128)(2,1)S(1)} %collective-permute-done.6.refs_2_, bf16[128,1024]{1,0:T(8,128)(2,1)S(1)} %collective-permute-done.7.refs_3_), custom_call_target="tpu_custom_call" | custom-call | bytes 2097152 | tf_op jit(solution)/shard_map/pallas_call | solution.py:152
  84.7 1.2 %fusion.6 = f32[1,256,512]{2,1,0:T(8,128)} fusion(f32[1,256,512]{2,1,0:T(8,128)S(1)} %copy-done.12, f32[256,512]{1,0:T(8,128)S(1)} %get-tuple-element.32, f32[512,512]{1,0:T(8,128)S(1)} %convert_element_type.13, bf16[256,512]{1,0:T(8,128)(2,1)S(1)} %collective-permute-done.9, f32[1,256,512]{2,1,0:T(8,128)S(1)} %copy-done.13, f32[1,256,512]{2,1,0:T(8,128)S(1)} %copy-done.11), kind=kLoop, calls=%fused_computation.10 | loop fusion | flops 2097152 | bytes 3407872 | tf_op jit(solution)/shard_map/broadcast_in_dim | solution.py:259
  (43 shorter events, 3.1 us)
Async XLA Ops:
  0.6 11.2 %copy-start = (bf16[1,128,4096]{2,1,0:T(8,128)(2,1)S(1)}, bf16[1,128,4096]{2,1,0:T(8,128)(2,1)}, u32[]{:S(2)}) copy-start(bf16[1,128,4096]{2,1,0:T(8,128)(2,1)} %param.9) | copy-start | bytes 3145732
  2.5 9.3 %copy-start.2 = (bf16[1,128,512]{2,1,0:T(8,128)(2,1)S(1)}, bf16[1,128,512]{2,1,0:T(8,128)(2,1)}, u32[]{:S(2)}) copy-start(bf16[1,128,512]{2,1,0:T(8,128)(2,1)} %param.10) | copy-start | bytes 393220
  2.5 24.6 %all-to-all-start = ((bf16[8,32,512]{2,1,0:T(8,128)(2,1)}), bf16[8,32,512]{2,1,0:T(8,128)(2,1)S(1)}, u32[]{:S(2)}, u32[]{:S(2)}) async-start(bf16[8,32,512]{2,1,0:T(8,128)(2,1)} %shard_map.128.after), calls=%async_computation | async-start | bytes 524288 | tf_op jit(solution)/shard_map/all_to_all | solution.py:187
  12.5 12.3 %copy-start.10 = (f32[1,256,512]{2,1,0:T(8,128)S(1)}, f32[1,256,512]{2,1,0:T(8,128)}, u32[]{:S(2)}) copy-start(f32[1,256,512]{2,1,0:T(8,128)} %param.11) | copy-start | bytes 1572868
  14.1 28.0 %collective-permute-start.1 = (bf16[128,1536]{1,0:T(8,128)(2,1)}, bf16[128,1536]{1,0:T(8,128)(2,1)S(1)}, u32[]{:S(2)}, u32[]{:S(2)}) collective-permute-start(bf16[128,1536]{1,0:T(8,128)(2,1)} %get-tuple-element.24), channel_id=1, source_target_pairs={{0,4},{1,5},{2,6},{3,7},{4,8},{5,9},{6,10},{7,11},{8,12},{9,13},{1... | collective-permute-start | bytes 1179656 | tf_op jit(solution)/shard_map/ppermute | solution.py:196
  17.3 24.8 %collective-permute-start.2 = (bf16[128,1536]{1,0:T(8,128)(2,1)}, bf16[128,1536]{1,0:T(8,128)(2,1)S(1)}, u32[]{:S(2)}, u32[]{:S(2)}) collective-permute-start(bf16[128,1536]{1,0:T(8,128)(2,1)} %get-tuple-element.25), channel_id=1, source_target_pairs={{0,8},{1,9},{2,10},{3,11},{4,12},{5,13},{6,14},{7,15},{8,0},{9,1},... | collective-permute-start | bytes 1179656 | tf_op jit(solution)/shard_map/ppermute | solution.py:196
  21.8 20.3 %collective-permute-start.3 = (bf16[128,1536]{1,0:T(8,128)(2,1)S(1)}, bf16[128,1536]{1,0:T(8,128)(2,1)S(1)}, u32[]{:S(2)}, u32[]{:S(2)}) collective-permute-start(bf16[128,1536]{1,0:T(8,128)(2,1)S(1)} %get-tuple-element.26), channel_id=1, source_target_pairs={{0,12},{1,13},{2,14},{3,15},{4,0},{5,1},{6,2},{7,3},{8,4},{9,5},{1... | collective-permute-start | bytes 1179656 | tf_op jit(solution)/shard_map/ppermute | solution.py:196
  24.8 2.3 %copy-start.3 = (f32[1,8,512]{2,1,0:T(8,128)S(1)}, f32[1,8,512]{2,1,0:T(8,128)}, u32[]{:S(2)}) copy-start(f32[1,8,512]{2,1,0:T(8,128)} %param.16) | copy-start | bytes 49156
  24.8 2.3 %copy-start.4 = (f32[1,8,512]{2,1,0:T(8,128)S(1)}, f32[1,8,512]{2,1,0:T(8,128)}, u32[]{:S(2)}) copy-start(f32[1,8,512]{2,1,0:T(8,128)} %param.17) | copy-start | bytes 49156
  24.9 17.2 %collective-permute-start = (bf16[256,512]{1,0:T(8,128)(2,1)S(1)}, bf16[256,512]{1,0:T(8,128)(2,1)S(1)}, u32[]{:S(2)}, u32[]{:S(2)}) collective-permute-start(bf16[256,512]{1,0:T(8,128)(2,1)S(1)} %convert_element_type.12.refs_1_), channel_id=1, source_target_pairs={{0,2},{1,3},{2,0},{3,1},{4,6},{5,7},{6,4},{7,5},{8,10},{9,11},{10,... | collective-permute-start | bytes 786440 | tf_op jit(solution)/shard_map/ppermute | solution.py:200
  27.8 21.2 %all-to-all-start.1 = ((bf16[4,48,512]{2,1,0:T(8,128)(2,1)}), bf16[4,48,512]{2,1,0:T(8,128)(2,1)S(1)}, u32[]{:S(2)}, u32[]{:S(2)}) async-start(bf16[4,48,512]{2,1,0:T(8,128)(2,1)} %shard_map.130), calls=%async_computation.1 | async-start | bytes 393216 | tf_op jit(solution)/shard_map/all_to_all | solution.py:210
  42.1 7.7 %collective-permute-start.4 = (bf16[512,512]{1,0:T(8,128)(2,1)S(1)}, bf16[512,512]{1,0:T(8,128)(2,1)S(1)}, u32[]{:S(2)}, u32[]{:S(2)}) collective-permute-start(bf16[512,512]{1,0:T(8,128)(2,1)S(1)} %pad_maximum_fusion), channel_id=1, source_target_pairs={{0,1},{1,0},{2,3},{3,2},{4,5},{5,4},{6,7},{7,6},{8,9},{9,8},{10,11... | collective-permute-start | bytes 1572872 | tf_op jit(solution)/shard_map/ppermute | solution.py:209
  51.3 1.4 %copy-start.8 = (bf16[128,1024]{1,0:T(8,128)(2,1)}, bf16[128,1024]{1,0:T(8,128)(2,1)S(1)}, u32[]{:S(2)}) copy-start(bf16[128,1024]{1,0:T(8,128)(2,1)S(1)} %get-tuple-element.29) | copy-start | bytes 786436
  52.7 12.2 %copy-start.9 = (bf16[128,1024]{1,0:T(8,128)(2,1)S(1)}, bf16[128,1024]{1,0:T(8,128)(2,1)}, u32[]{:S(2)}) copy-start(bf16[128,1024]{1,0:T(8,128)(2,1)} %copy-done.8) | copy-start | bytes 786436
  52.7 14.1 %copy-start.7 = (bf16[128,1024]{1,0:T(8,128)(2,1)S(1)}, bf16[128,1024]{1,0:T(8,128)(2,1)}, u32[]{:S(2)}) copy-start(bf16[128,1024]{1,0:T(8,128)(2,1)} %copy-done.6) | copy-start | bytes 786436
  52.7 20.2 %collective-permute-start.8 = (bf16[512,512]{1,0:T(8,128)(2,1)}, bf16[512,512]{1,0:T(8,128)(2,1)S(1)}, u32[]{:S(2)}, u32[]{:S(2)}) collective-permute-start(bf16[512,512]{1,0:T(8,128)(2,1)} %get-tuple-element.33), channel_id=1, source_target_pairs={{0,1},{1,0},{2,3},{3,2},{4,5},{5,4},{6,7},{7,6},{8,9},{9,8},{10,11... | collective-permute-start | bytes 1572872 | tf_op jit(solution)/shard_map/ppermute | solution.py:240
  57.6 28.3 %all-to-all-start.2 = ((bf16[8,32,512]{2,1,0:T(8,128)(2,1)}), bf16[8,32,512]{2,1,0:T(8,128)(2,1)S(1)}, u32[]{:S(2)}, u32[]{:S(2)}) async-start(bf16[8,32,512]{2,1,0:T(8,128)(2,1)} %get-tuple-element.22.refs_0_), calls=%async_computation.2 | async-start | bytes 524288 | tf_op jit(solution)/shard_map/all_to_all | solution.py:217
  64.9 10.3 %collective-permute-start.5 = (bf16[128,1024]{1,0:T(8,128)(2,1)S(1)}, bf16[128,1024]{1,0:T(8,128)(2,1)S(1)}, u32[]{:S(2)}, u32[]{:S(2)}) collective-permute-start(bf16[128,1024]{1,0:T(8,128)(2,1)S(1)} %copy-done.9), channel_id=1, source_target_pairs={{0,12},{1,13},{2,14},{3,15},{4,0},{5,1},{6,2},{7,3},{8,4},{9,5},{1... | collective-permute-start | bytes 786440 | tf_op jit(solution)/shard_map/ppermute | solution.py:230
  66.8 10.4 %collective-permute-start.6 = (bf16[128,1024]{1,0:T(8,128)(2,1)S(1)}, bf16[128,1024]{1,0:T(8,128)(2,1)S(1)}, u32[]{:S(2)}, u32[]{:S(2)}) collective-permute-start(bf16[128,1024]{1,0:T(8,128)(2,1)S(1)} %copy-done.7), channel_id=1, source_target_pairs={{0,8},{1,9},{2,10},{3,11},{4,12},{5,13},{6,14},{7,15},{8,0},{9,1},... | collective-permute-start | bytes 786440 | tf_op jit(solution)/shard_map/ppermute | solution.py:230
  70.9 12.6 %collective-permute-start.7 = (bf16[128,1024]{1,0:T(8,128)(2,1)S(1)}, bf16[128,1024]{1,0:T(8,128)(2,1)S(1)}, u32[]{:S(2)}, u32[]{:S(2)}) collective-permute-start(bf16[128,1024]{1,0:T(8,128)(2,1)S(1)} %get-tuple-element.31), channel_id=1, source_target_pairs={{0,4},{1,5},{2,6},{3,7},{4,8},{5,9},{6,10},{7,11},{8,12},{9,13},{1... | collective-permute-start | bytes 786440 | tf_op jit(solution)/shard_map/ppermute | solution.py:230
  73.1 11.6 %copy-start.11 = (f32[1,256,512]{2,1,0:T(8,128)S(1)}, f32[1,256,512]{2,1,0:T(8,128)}, u32[]{:S(2)}) copy-start(f32[1,256,512]{2,1,0:T(8,128)} %param.11) | copy-start | bytes 1572868
  73.1 11.6 %copy-start.12 = (f32[1,256,512]{2,1,0:T(8,128)S(1)}, f32[1,256,512]{2,1,0:T(8,128)}, u32[]{:S(2)}) copy-start(f32[1,256,512]{2,1,0:T(8,128)} %param.13) | copy-start | bytes 1572868
  73.1 11.5 %copy-start.13 = (f32[1,256,512]{2,1,0:T(8,128)S(1)}, f32[1,256,512]{2,1,0:T(8,128)}, u32[]{:S(2)}) copy-start(f32[1,256,512]{2,1,0:T(8,128)} %param.12) | copy-start | bytes 1572868
  73.1 11.5 %collective-permute-start.9 = (bf16[256,512]{1,0:T(8,128)(2,1)S(1)}, bf16[256,512]{1,0:T(8,128)(2,1)S(1)}, u32[]{:S(2)}, u32[]{:S(2)}) collective-permute-start(bf16[256,512]{1,0:T(8,128)(2,1)S(1)} %fusion), channel_id=1, source_target_pairs={{0,2},{1,3},{2,0},{3,1},{4,6},{5,7},{6,4},{7,5},{8,10},{9,11},{10,... | collective-permute-start | bytes 786440 | tf_op jit(solution)/shard_map/ppermute | solution.py:241
  (3 other events, 2.5 us)

commit v4 on v3

--- a/solution.py
+++ b/solution.py
@@ -11,7 +11,7 @@
 COLUMN = 4
 SIDES = 2
 NEAR = SIDES * QUAD
-NEAR_ORDER = ((0, 1), (0, 2), (0, 0), (0, 3), (1, 1), (1, 2), (1, 0), (1, 3))
+NEAR_ORDER = ((1, 1), (1, 2), (0, 1), (0, 2), (1, 0), (1, 3), (0, 0), (0, 3))
 FAR_ORDER = (2, 3, 1, 0)
 HALF = jnp.bfloat16
 FULL = jnp.float32
@@ -58,7 +58,7 @@
         packed[d][:, QUAD * block :] = masked
 
 
-def sum_kernel(pieces, anchor, momentum, after, sums):
+def sum_kernel(pieces, anchor, momentum, after, later, sums):
     total = pieces[0].astype(FULL)
     for i in range(1, NEAR):
         total += pieces[i].astype(FULL)
@@ -92,7 +92,8 @@
 
 
 def input_kernel(factor, after, own, beside, across, *refs):
-    cotangents, results = refs[:COLUMN], refs[COLUMN:]
+    cotangents, results = refs[:COLUMN], refs[COLUMN]
+    y = lax.axis_index("fsdp") // QUAD
     tokens = cotangents[0].shape[0]
     block = own.shape[0]
     left = jnp.concatenate([ref[...] for ref in cotangents], axis=0)
@@ -100,7 +101,8 @@
         product = lax.dot_general(left, right, (((1,), (1,)), ((), ())), preferred_element_type=FULL)
         product = (product * factor).astype(HALF)
         for d in range(COLUMN):
-            results[d][:, step * block : (step + 1) * block] = product[d * tokens : (d + 1) * tokens]
+            part = product[d * tokens : (d + 1) * tokens]
+            results[(y + COLUMN - d) % COLUMN, :, step * block : (step + 1) * block] = part
 
 
 def weight_kernel(*refs):
@@ -122,17 +124,16 @@
 
 
 def unpack_kernel(*refs):
-    pieces, result, done = refs[:COLUMN], refs[COLUMN], refs[COLUMN + 1]
-    me = lax.axis_index("fsdp")
-    place, y = me % QUAD, me // QUAD
+    pieces, result, done = refs
+    place = lax.axis_index("fsdp") % QUAD
     block = result.shape[1] // (COLUMN * QUAD)
     copies = []
     for d in range(COLUMN):
         for step in range(QUAD):
-            target = ((y + d) % COLUMN * QUAD + block_of(place, step)) * block
+            target = (d * QUAD + block_of(place, step)) * block
             copies.append(
                 pltpu.make_async_copy(
-                    pieces[d].at[:, pl.ds(step * block, block)],
+                    pieces.at[d, :, pl.ds(step * block, block)],
                     result.at[:, pl.ds(pl.multiple_of(target, block), block)],
                     done.at[d * QUAD + step],
                 )
@@ -177,7 +178,7 @@
     beside = [(f, f ^ 2) for f in range(shards)]
     across = [(f, f ^ 1) for f in range(shards)]
     up = [[(f, (f + QUAD * d) % shards) for f in range(shards)] for d in range(COLUMN)]
-    down = [[(f, (f - QUAD * d) % shards) for f in range(shards)] for d in range(COLUMN)]
+    columns = [[QUAD * y + j for y in range(COLUMN)] for j in range(QUAD)]
     depth = replicas // SIDES
     outer = depth // QUAD
     near = [[depth * h + QUAD * a + b for h, b in NEAR_ORDER] for a in range(outer)]
@@ -202,10 +203,10 @@
     (sums,) = call(
         sum_kernel,
         [((outer, (outer + 2) * share, keys), HALF)],
-        (near_pieces, anchor[0], momentum[0], packed[0]),
-        [VMEM, VMEM, VMEM, ANY],
-    )
-    other = lax.optimization_barrier((other, sums, packed[1], packed[2], packed[3]))[0]
+        (near_pieces, anchor[0], momentum[0], packed[0], other),
+        [VMEM, VMEM, VMEM, ANY, ANY],
+    )
+    other = lax.optimization_barrier((other, sums, packed[2], packed[3]))[0]
     both = lax.ppermute(jnp.concatenate([own, other], axis=0), "fsdp", across)
     sums = lax.all_to_all(sums, "replica", 0, 0, axis_index_groups=far)
     anchor_out, momentum_out, fresh = call(
@@ -214,32 +215,33 @@
         (sums, anchor[0], momentum[0]),
         scratch=[pltpu.VMEM((outer * share, keys), FULL)],
     )
-    spread = lax.all_to_all(fresh, "replica", 0, 0, axis_index_groups=near)
-    (spread,) = call(join_kernel, [(pseudo_grad.shape[2:], HALF)], (spread,))
 
     cot_spec = pl.BlockSpec((tokens, keys), lambda *_: (0, wide // keys))
-    products = call(
+    (products,) = call(
         lambda *refs: input_kernel(factor, *refs),
-        [((tokens, wide), HALF)] * COLUMN,
+        [((COLUMN, tokens, wide), HALF)],
         (fresh, own, other, both, *packed),
         [ANY, whole(own.shape), whole(own.shape), whole(both.shape)] + [cot_spec] * COLUMN,
         flops=flops,
         moved=3 << 20,
         grid=(1,),
     )
-    back = [products[0]] + [lax.ppermute(products[d], "fsdp", down[d]) for d in (1, 2, 3)]
+    spread = lax.all_to_all(fresh, "replica", 0, 0, axis_index_groups=near)
+    outgoing, spread = lax.optimization_barrier((products, spread))
+    back = lax.all_to_all(outgoing, "fsdp", 0, 0, axis_index_groups=columns)
+    (spread,) = call(join_kernel, [(pseudo_grad.shape[2:], HALF)], (spread,))
 
     grad_own, grad_passed, sent = call(
         weight_kernel,
         [((rows, keys), FULL), ((rows, keys), FULL), ((2 * rows, keys), HALF)],
-        (*packed, products[0]),
+        (*packed, products),
         [VMEM] * COLUMN + [ANY],
         flops=flops,
         moved=5 << 20,
     )
-    crossed = lax.ppermute(sent, "fsdp", across).astype(FULL)
-    passed = lax.ppermute((grad_passed + crossed[rows:]).astype(HALF), "fsdp", beside)
-    summed = grad_own + crossed[:rows] + passed.astype(FULL)
+    crossed = lax.ppermute(sent, "fsdp", across)
+    passed = lax.ppermute((grad_passed + crossed[rows:].astype(FULL)).astype(HALF), "fsdp", beside)
+    summed = grad_own + crossed[:rows].astype(FULL) + passed.astype(FULL)
 
     grad = summed * factor
     first = 0.9 * moment_one[0] + 0.1 * grad
@@ -249,8 +251,8 @@
     (input_grad,) = call(
         unpack_kernel,
         [((tokens, width), HALF)],
-        back,
-        [ANY] * COLUMN,
+        (back,),
+        [ANY],
         [ANY],
         scratch=[pltpu.SemaphoreType.DMA((COLUMN * QUAD,))],
         moved=2 << 20,

time: 87.4 us -> 85.3 us (0.976)
  starting transfers between devices: 63.5 us -> 55.6 us
  waiting for transfers between devices: 10.5 us -> 14.4 us
  other arithmetic: 1.5 us -> 3.2 us
  Pallas kernels: 7.73 us -> 8.62 us
    ppermute x5 -> x2, starting transfers between devices: 14.9 us -> 5.64 us  [the longest x1 2.95 us: local(): lax.ppermute((grad_passed + crossed[rows:].astype(FULL)).astype(HALF), 'f...]
    all_to_all x0 -> x1, starting transfers between devices: none -> 3.53 us  [local(): back = lax.all_to_all(outgoing, 'fsdp', 0, 0, axis_index_groups=columns)]
    ppermute x3, waiting for transfers between devices: 0.01 us -> 3.36 us  [local(): lax.ppermute(packed[d], 'fsdp', up[d])]
    all_to_all x0 -> x1, waiting for transfers between devices: none -> 2.16 us  [local(): back = lax.all_to_all(outgoing, 'fsdp', 0, 0, axis_index_groups=columns)]
    all_to_all x1, starting transfers between devices: 7.28 us -> 5.14 us  [local(): spread = lax.all_to_all(fresh, 'replica', 0, 0, axis_index_groups=near)]
    ppermute x5 -> x2, waiting for transfers between devices: 8.35 us -> 7 us  [the longest x1 7 us: local(): lax.ppermute((grad_passed + crossed[rows:].astype(FULL)).astype(HALF), 'f...]
    broadcast_in_dim x1, other arithmetic: 1.22 us -> 2.27 us  [local(): master_out[None]]
    pallas_call x8, Pallas kernels: 7.73 us -> 8.62 us  [call(): pl.pallas_call(kernel, grid=grid, out_shape=outs, in_specs=in_specs or [V...]
  transfers between devices with their start and end apart: 13 -> 11, of which waited for: 3 -> 4; matrix products, arithmetic and copies ran while one was open for 2% -> 4% of each run, Pallas kernels for 5% -> 8%
where the time goes in v4:
time: 85.3 us; the launch traced here: 84.5 us
  starting transfers between devices  55.6 us (65%)
  waiting for transfers between devices  14.4 us (17%)
  Pallas kernels  8.62 us (10%)
  other arithmetic  3.2 us (4%)
  local copies, waits for them, and re-layouts  1.8 us (2%)
    all_to_all x1, starting transfers between devices, local(): sums = lax.all_to_all(sums, 'replica', 0, 0, axis_index_groups=far)  14.4 us
    ppermute x3, starting transfers between devices, local(): lax.ppermute(packed[d], 'fsdp', up[d])  10.2 us
    all_to_all x1, starting transfers between devices, local(): lax.all_to_all(pieces, 'replica', 0, 0, axis_index_groups=near)  9.32 us
    pallas_call x8, Pallas kernels, call(): pl.pallas_call(kernel, grid=grid, out_shape=outs, in_specs=in_specs or [V...  8.62 us
    ppermute x1, waiting for transfers between devices, local(): lax.ppermute((grad_passed + crossed[rows:].astype(FULL)).astype(HALF), 'f...  7 us
    all_to_all x1, starting transfers between devices, local(): spread = lax.all_to_all(fresh, 'replica', 0, 0, axis_index_groups=near)  5.14 us
    ppermute x1, starting transfers between devices, local(): both = lax.ppermute(jnp.concatenate([own, other], axis=0), 'fsdp', across)  4.36 us
    all_to_all x1, starting transfers between devices, local(): back = lax.all_to_all(outgoing, 'fsdp', 0, 0, axis_index_groups=columns)  3.53 us
  transfers between devices with their start and end apart: 11, of which 4 were waited for; matrix products, arithmetic and copies ran while one was open for 4% of the time, Pallas kernels for 8%

profile of v4, /device:TPU:1, one launch (start us, length us, event | category | flops | bytes accessed | tf_op | source)
XLA Modules:
  0.0 84.5 jit_solution(8407197766471024948)
XLA Ops:
  0.7 1.1 %copy-done.1 = f32[1,1,256,512]{3,2,1,0:T(8,128)S(1)} copy-done((f32[1,1,256,512]{3,2,1,0:T(8,128)S(1)}, f32[1,1,256,512]{3,2,1,0:T(8,128)}, u32[]{:S(2)}) %copy-start.1) | copy-done | bytes 524312
  1.8 0.7 shard_map.128.after
  2.5 9.3 %all-to-all-start = ((bf16[8,32,512]{2,1,0:T(8,128)(2,1)}), bf16[8,32,512]{2,1,0:T(8,128)(2,1)S(1)}, u32[]{:S(2)}, u32[]{:S(2)}) async-start(bf16[8,32,512]{2,1,0:T(8,128)(2,1)} %shard_map.128.after), calls=%async_computation | async-start | bytes 524288 | tf_op jit(solution)/shard_map/all_to_all | solution.py:188
  12.5 1.4 %shard_map.129 = (bf16[128,1536]{1,0:T(8,128)(2,1)S(1)}, bf16[128,1536]{1,0:T(8,128)(2,1)S(1)}, bf16[128,1536]{1,0:T(8,128)(2,1)}, bf16[128,1536]{1,0:T(8,128)(2,1)S(1)}) custom-call(s32[1,16]{1,0:T(1,128)S(1)} %copy-done.5, bf16[128,4096]{1,0:T(8,128)(2,1)S(1)} %bitcast.31, bf16[128,512]{1,0:T(8,128)(2,1)S(1)} %bitcast.33, bf16[8,32,512]{2,1,0:T(8,128)(2,1)} %shard_map.128.after), custom_call_target="tpu_custom_call" | custom-call | bytes 3145728 | tf_op jit(solution)/shard_map/pallas_call | solution.py:153
  14.0 3.1 %collective-permute-start = (bf16[256,512]{1,0:T(8,128)(2,1)S(1)}, bf16[256,512]{1,0:T(8,128)(2,1)S(1)}, u32[]{:S(2)}, u32[]{:S(2)}) collective-permute-start(bf16[256,512]{1,0:T(8,128)(2,1)S(1)} %convert_element_type.15.refs_1_), channel_id=1, source_target_pairs={{0,2},{1,3},{2,0},{3,1},{4,6},{5,7},{6,4},{7,5},{8,10},{9,11},{10,... | collective-permute-start | bytes 786440 | tf_op jit(solution)/shard_map/ppermute | solution.py:201
  17.0 4.8 %collective-permute-start.1 = (bf16[128,1536]{1,0:T(8,128)(2,1)}, bf16[128,1536]{1,0:T(8,128)(2,1)S(1)}, u32[]{:S(2)}, u32[]{:S(2)}) collective-permute-start(bf16[128,1536]{1,0:T(8,128)(2,1)} %get-tuple-element.22), channel_id=1, source_target_pairs={{0,8},{1,9},{2,10},{3,11},{4,12},{5,13},{6,14},{7,15},{8,0},{9,1},... | collective-permute-start | bytes 1179656 | tf_op jit(solution)/shard_map/ppermute | solution.py:197
  21.9 2.7 %collective-permute-start.2 = (bf16[128,1536]{1,0:T(8,128)(2,1)S(1)}, bf16[128,1536]{1,0:T(8,128)(2,1)S(1)}, u32[]{:S(2)}, u32[]{:S(2)}) collective-permute-start(bf16[128,1536]{1,0:T(8,128)(2,1)S(1)} %get-tuple-element.23), channel_id=1, source_target_pairs={{0,12},{1,13},{2,14},{3,15},{4,0},{5,1},{6,2},{7,3},{8,4},{9,5},{1... | collective-permute-start | bytes 1179656 | tf_op jit(solution)/shard_map/ppermute | solution.py:197
  25.3 14.4 %all-to-all-start.1 = ((bf16[4,48,512]{2,1,0:T(8,128)(2,1)}), bf16[4,48,512]{2,1,0:T(8,128)(2,1)S(1)}, u32[]{:S(2)}, u32[]{:S(2)}) async-start(bf16[4,48,512]{2,1,0:T(8,128)(2,1)} %shard_map.130), calls=%async_computation.1 | async-start | bytes 393216 | tf_op jit(solution)/shard_map/all_to_all | solution.py:211
  39.7 0.8 pad_maximum_fusion
  40.5 4.4 %collective-permute-start.3 = (bf16[512,512]{1,0:T(8,128)(2,1)}, bf16[512,512]{1,0:T(8,128)(2,1)S(1)}, u32[]{:S(2)}, u32[]{:S(2)}) collective-permute-start(bf16[512,512]{1,0:T(8,128)(2,1)} %pad_maximum_fusion), channel_id=1, source_target_pairs={{0,1},{1,0},{2,3},{3,2},{4,5},{5,4},{6,7},{7,6},{8,9},{9,8},{10,11... | collective-permute-start | bytes 1572872 | tf_op jit(solution)/shard_map/ppermute | solution.py:210
  44.9 2.7 %collective-permute-start.4 = (bf16[128,1536]{1,0:T(8,128)(2,1)S(1)}, bf16[128,1536]{1,0:T(8,128)(2,1)S(1)}, u32[]{:S(2)}, u32[]{:S(2)}) collective-permute-start(bf16[128,1536]{1,0:T(8,128)(2,1)S(1)} %get-tuple-element.25), channel_id=1, source_target_pairs={{0,4},{1,5},{2,6},{3,7},{4,8},{5,9},{6,10},{7,11},{8,12},{9,13},{1... | collective-permute-start | bytes 1179656 | tf_op jit(solution)/shard_map/ppermute | solution.py:197
  47.6 1.9 %all-to-all-done.1.sums = bf16[4,48,512]{2,1,0:T(8,128)(2,1)S(1)} async-done(((bf16[4,48,512]{2,1,0:T(8,128)(2,1)}), bf16[4,48,512]{2,1,0:T(8,128)(2,1)S(1)}, u32[]{:S(2)}, u32[]{:S(2)}) %all-to-all-start.1) | async-done | bytes 196640 | tf_op jit(solution)/shard_map/all_to_all | solution.py:211
  49.5 0.8 shard_map.131
  50.3 5.1 %all-to-all-start.2 = ((bf16[8,32,512]{2,1,0:T(8,128)(2,1)}), bf16[8,32,512]{2,1,0:T(8,128)(2,1)S(1)}, u32[]{:S(2)}, u32[]{:S(2)}) async-start(bf16[8,32,512]{2,1,0:T(8,128)(2,1)} %get-tuple-element.21.refs_0_), calls=%async_computation.2 | async-start | bytes 524288 | tf_op jit(solution)/shard_map/all_to_all | solution.py:229
  55.4 3.4 %collective-permute-done.4.refs_5_.refs_1_ = bf16[128,1536]{1,0:T(8,128)(2,1)S(1)} collective-permute-done((bf16[128,1536]{1,0:T(8,128)(2,1)S(1)}, bf16[128,1536]{1,0:T(8,128)(2,1)S(1)}, u32[]{:S(2)}, u32[]{:S(2)}) %collective-permute-start.4) | collective-permute-done | bytes 393248 | tf_op jit(solution)/shard_map/ppermute | solution.py:197
  58.8 1.8 %shard_map.132.refs_4_ = bf16[4,128,1024]{2,1,0:T(8,128)(2,1)} custom-call(bf16[8,32,512]{2,1,0:T(8,128)(2,1)} %get-tuple-element.21.refs_0_, bf16[256,512]{1,0:T(8,128)(2,1)S(1)} %convert_element_type.15.refs_1_, bf16[256,512]{1,0:T(8,128)(2,1)S(1)} %collective-permute-done.later.refs_2_, bf16[512,512]{1,0:T(8,128)(2,1)S(1)} %collective-permute-done.3.refs_3_, ...), custom_call_target="tpu_custom_call" | custom-call | flops 536870912 | bytes 3145728 | tf_op jit(solution)/shard_map/pallas_call | solution.py:153
  60.5 1.4 %shard_map.134 = (f32[256,512]{1,0:T(8,128)S(1)}, f32[256,512]{1,0:T(8,128)S(1)}, bf16[512,512]{1,0:T(8,128)(2,1)}) custom-call(bf16[128,1536]{1,0:T(8,128)(2,1)S(1)} %get-tuple-element.19.after.refs_4_.refs_0_, bf16[128,1536]{1,0:T(8,128)(2,1)S(1)} %collective-permute-done.4.refs_5_.refs_1_, bf16[128,1536]{1,0:T(8,128)(2,1)S(1)} %collective-permute-done.1.refs_6_.refs_2_, ...), custom_call_target="tpu_custom_call" | custom-call | flops 536870912 | bytes 5242880 | tf_op jit(solution)/shard_map/pallas_call | solution.py:153
  61.9 2.7 %collective-permute-start.5 = (bf16[512,512]{1,0:T(8,128)(2,1)}, bf16[512,512]{1,0:T(8,128)(2,1)S(1)}, u32[]{:S(2)}, u32[]{:S(2)}) collective-permute-start(bf16[512,512]{1,0:T(8,128)(2,1)} %get-tuple-element.28), channel_id=1, source_target_pairs={{0,1},{1,0},{2,3},{3,2},{4,5},{5,4},{6,7},{7,6},{8,9},{9,8},{10,11... | collective-permute-start | bytes 1572872 | tf_op jit(solution)/shard_map/ppermute | solution.py:242
  64.6 3.5 %all-to-all-start.3 = ((bf16[4,128,1024]{2,1,0:T(8,128)(2,1)}), bf16[4,128,1024]{2,1,0:T(8,128)(2,1)S(1)}, u32[]{:S(2)}, u32[]{:S(2)}) async-start(bf16[4,128,1024]{2,1,0:T(8,128)(2,1)} %shard_map.132.refs_4_), calls=%async_computation.3 | async-start | bytes 2097152 | tf_op jit(solution)/shard_map/all_to_all | solution.py:231
  68.3 2.9 %collective-permute-start.6 = (bf16[256,512]{1,0:T(8,128)(2,1)S(1)}, bf16[256,512]{1,0:T(8,128)(2,1)S(1)}, u32[]{:S(2)}, u32[]{:S(2)}) collective-permute-start(bf16[256,512]{1,0:T(8,128)(2,1)S(1)} %add_convert_fusion), channel_id=1, source_target_pairs={{0,2},{1,3},{2,0},{3,1},{4,6},{5,7},{6,4},{7,5},{8,10},{9,11},{10,... | collective-permute-start | bytes 786440 | tf_op jit(solution)/shard_map/ppermute | solution.py:243
  71.2 7.0 %collective-permute-done.6 = bf16[256,512]{1,0:T(8,128)(2,1)S(1)} collective-permute-done((bf16[256,512]{1,0:T(8,128)(2,1)S(1)}, bf16[256,512]{1,0:T(8,128)(2,1)S(1)}, u32[]{:S(2)}, u32[]{:S(2)}) %collective-permute-start.6) | collective-permute-done | bytes 262176 | tf_op jit(solution)/shard_map/ppermute | solution.py:243
  78.2 2.3 %fusion.4 = f32[1,256,512]{2,1,0:T(8,128)} fusion(f32[1,256,512]{2,1,0:T(8,128)S(1)} %copy-done.8, bf16[256,512]{1,0:T(8,128)(2,1)S(1)} %collective-permute-done.6, f32[256,512]{1,0:T(8,128)S(1)} %get-tuple-element.27, f32[1,256,512]{2,1,0:T(8,128)} %param.12, bf16[512,512]{1,0:T(8,128)(2,1)S(1)} %collective-permute-done.5, f32[1,256,512]{2,1,0:T(8,128)S(1)} %copy-done.7), kind=kLoop, calls=%fused_computation.6 | loop fusion | flops 2228224 | bytes 3145728 | tf_op jit(solution)/shard_map/broadcast_in_dim | solution.py:261
  81.2 2.2 %all-to-all-done.3.refs_0_ = bf16[4,128,1024]{2,1,0:T(8,128)(2,1)S(1)} async-done(((bf16[4,128,1024]{2,1,0:T(8,128)(2,1)}), bf16[4,128,1024]{2,1,0:T(8,128)(2,1)S(1)}, u32[]{:S(2)}, u32[]{:S(2)}) %all-to-all-start.3) | async-done | bytes 1048608 | tf_op jit(solution)/shard_map/all_to_all | solution.py:231
  83.4 1.1 %shard_map.133 = bf16[128,4096]{1,0:T(8,128)(2,1)} custom-call(bf16[4,128,1024]{2,1,0:T(8,128)(2,1)S(1)} %all-to-all-done.3.refs_0_), custom_call_target="tpu_custom_call" | custom-call | bytes 2097152 | tf_op jit(solution)/shard_map/pallas_call | solution.py:153
  (28 shorter events, 2.2 us)
Async XLA Ops:
  0.6 11.2 %copy-start = (bf16[1,128,4096]{2,1,0:T(8,128)(2,1)S(1)}, bf16[1,128,4096]{2,1,0:T(8,128)(2,1)}, u32[]{:S(2)}) copy-start(bf16[1,128,4096]{2,1,0:T(8,128)(2,1)} %param.9) | copy-start | bytes 3145732
  0.6 1.1 %copy-start.1 = (f32[1,1,256,512]{3,2,1,0:T(8,128)S(1)}, f32[1,1,256,512]{3,2,1,0:T(8,128)}, u32[]{:S(2)}) copy-start(f32[1,1,256,512]{3,2,1,0:T(8,128)} %param.15) | copy-start | bytes 1572868
  2.5 9.3 %copy-start.2 = (bf16[1,128,512]{2,1,0:T(8,128)(2,1)S(1)}, bf16[1,128,512]{2,1,0:T(8,128)(2,1)}, u32[]{:S(2)}) copy-start(bf16[1,128,512]{2,1,0:T(8,128)(2,1)} %param.10) | copy-start | bytes 393220
  2.5 22.1 %all-to-all-start = ((bf16[8,32,512]{2,1,0:T(8,128)(2,1)}), bf16[8,32,512]{2,1,0:T(8,128)(2,1)S(1)}, u32[]{:S(2)}, u32[]{:S(2)}) async-start(bf16[8,32,512]{2,1,0:T(8,128)(2,1)} %shard_map.128.after), calls=%async_computation | async-start | bytes 524288 | tf_op jit(solution)/shard_map/all_to_all | solution.py:188
  11.8 0.7 copy-start.5
  12.5 1.4 %copy-start.6 = (f32[1,256,512]{2,1,0:T(8,128)S(1)}, f32[1,256,512]{2,1,0:T(8,128)}, u32[]{:S(2)}) copy-start(f32[1,256,512]{2,1,0:T(8,128)} %param.11) | copy-start | bytes 1572868
  13.9 10.7 %copy-start.3 = (f32[1,8,512]{2,1,0:T(8,128)S(1)}, f32[1,8,512]{2,1,0:T(8,128)}, u32[]{:S(2)}) copy-start(f32[1,8,512]{2,1,0:T(8,128)} %param.16) | copy-start | bytes 49156
  13.9 10.7 %copy-start.4 = (f32[1,8,512]{2,1,0:T(8,128)S(1)}, f32[1,8,512]{2,1,0:T(8,128)}, u32[]{:S(2)}) copy-start(f32[1,8,512]{2,1,0:T(8,128)} %param.17) | copy-start | bytes 49156
  14.0 10.6 %collective-permute-start = (bf16[256,512]{1,0:T(8,128)(2,1)S(1)}, bf16[256,512]{1,0:T(8,128)(2,1)S(1)}, u32[]{:S(2)}, u32[]{:S(2)}) collective-permute-start(bf16[256,512]{1,0:T(8,128)(2,1)S(1)} %convert_element_type.15.refs_1_), channel_id=1, source_target_pairs={{0,2},{1,3},{2,0},{3,1},{4,6},{5,7},{6,4},{7,5},{8,10},{9,11},{10,... | collective-permute-start | bytes 786440 | tf_op jit(solution)/shard_map/ppermute | solution.py:201
  17.0 22.7 %collective-permute-start.1 = (bf16[128,1536]{1,0:T(8,128)(2,1)}, bf16[128,1536]{1,0:T(8,128)(2,1)S(1)}, u32[]{:S(2)}, u32[]{:S(2)}) collective-permute-start(bf16[128,1536]{1,0:T(8,128)(2,1)} %get-tuple-element.22), channel_id=1, source_target_pairs={{0,8},{1,9},{2,10},{3,11},{4,12},{5,13},{6,14},{7,15},{8,0},{9,1},... | collective-permute-start | bytes 1179656 | tf_op jit(solution)/shard_map/ppermute | solution.py:197
  21.9 17.8 %collective-permute-start.2 = (bf16[128,1536]{1,0:T(8,128)(2,1)S(1)}, bf16[128,1536]{1,0:T(8,128)(2,1)S(1)}, u32[]{:S(2)}, u32[]{:S(2)}) collective-permute-start(bf16[128,1536]{1,0:T(8,128)(2,1)S(1)} %get-tuple-element.23), channel_id=1, source_target_pairs={{0,12},{1,13},{2,14},{3,15},{4,0},{5,1},{6,2},{7,3},{8,4},{9,5},{1... | collective-permute-start | bytes 1179656 | tf_op jit(solution)/shard_map/ppermute | solution.py:197
  25.3 24.2 %all-to-all-start.1 = ((bf16[4,48,512]{2,1,0:T(8,128)(2,1)}), bf16[4,48,512]{2,1,0:T(8,128)(2,1)S(1)}, u32[]{:S(2)}, u32[]{:S(2)}) async-start(bf16[4,48,512]{2,1,0:T(8,128)(2,1)} %shard_map.130), calls=%async_computation.1 | async-start | bytes 393216 | tf_op jit(solution)/shard_map/all_to_all | solution.py:211
  40.5 18.2 %collective-permute-start.3 = (bf16[512,512]{1,0:T(8,128)(2,1)}, bf16[512,512]{1,0:T(8,128)(2,1)S(1)}, u32[]{:S(2)}, u32[]{:S(2)}) collective-permute-start(bf16[512,512]{1,0:T(8,128)(2,1)} %pad_maximum_fusion), channel_id=1, source_target_pairs={{0,1},{1,0},{2,3},{3,2},{4,5},{5,4},{6,7},{7,6},{8,9},{9,8},{10,11... | collective-permute-start | bytes 1572872 | tf_op jit(solution)/shard_map/ppermute | solution.py:210
  44.9 13.8 %collective-permute-start.4 = (bf16[128,1536]{1,0:T(8,128)(2,1)S(1)}, bf16[128,1536]{1,0:T(8,128)(2,1)S(1)}, u32[]{:S(2)}, u32[]{:S(2)}) collective-permute-start(bf16[128,1536]{1,0:T(8,128)(2,1)S(1)} %get-tuple-element.25), channel_id=1, source_target_pairs={{0,4},{1,5},{2,6},{3,7},{4,8},{5,9},{6,10},{7,11},{8,12},{9,13},{1... | collective-permute-start | bytes 1179656 | tf_op jit(solution)/shard_map/ppermute | solution.py:197
  50.3 14.4 %all-to-all-start.2 = ((bf16[8,32,512]{2,1,0:T(8,128)(2,1)}), bf16[8,32,512]{2,1,0:T(8,128)(2,1)S(1)}, u32[]{:S(2)}, u32[]{:S(2)}) async-start(bf16[8,32,512]{2,1,0:T(8,128)(2,1)} %get-tuple-element.21.refs_0_), calls=%async_computation.2 | async-start | bytes 524288 | tf_op jit(solution)/shard_map/all_to_all | solution.py:229
  61.9 6.3 %collective-permute-start.5 = (bf16[512,512]{1,0:T(8,128)(2,1)}, bf16[512,512]{1,0:T(8,128)(2,1)S(1)}, u32[]{:S(2)}, u32[]{:S(2)}) collective-permute-start(bf16[512,512]{1,0:T(8,128)(2,1)} %get-tuple-element.28), channel_id=1, source_target_pairs={{0,1},{1,0},{2,3},{3,2},{4,5},{5,4},{6,7},{7,6},{8,9},{9,8},{10,11... | collective-permute-start | bytes 1572872 | tf_op jit(solution)/shard_map/ppermute | solution.py:242
  64.6 18.8 %all-to-all-start.3 = ((bf16[4,128,1024]{2,1,0:T(8,128)(2,1)}), bf16[4,128,1024]{2,1,0:T(8,128)(2,1)S(1)}, u32[]{:S(2)}, u32[]{:S(2)}) async-start(bf16[4,128,1024]{2,1,0:T(8,128)(2,1)} %shard_map.132.refs_4_), calls=%async_computation.3 | async-start | bytes 2097152 | tf_op jit(solution)/shard_map/all_to_all | solution.py:231
  68.2 10.1 %copy-start.7 = (f32[1,256,512]{2,1,0:T(8,128)S(1)}, f32[1,256,512]{2,1,0:T(8,128)}, u32[]{:S(2)}) copy-start(f32[1,256,512]{2,1,0:T(8,128)} %param.11) | copy-start | bytes 1572868
  68.2 10.0 %copy-start.8 = (f32[1,256,512]{2,1,0:T(8,128)S(1)}, f32[1,256,512]{2,1,0:T(8,128)}, u32[]{:S(2)}) copy-start(f32[1,256,512]{2,1,0:T(8,128)} %param.13) | copy-start | bytes 1572868
  68.3 10.0 %collective-permute-start.6 = (bf16[256,512]{1,0:T(8,128)(2,1)S(1)}, bf16[256,512]{1,0:T(8,128)(2,1)S(1)}, u32[]{:S(2)}, u32[]{:S(2)}) collective-permute-start(bf16[256,512]{1,0:T(8,128)(2,1)S(1)} %add_convert_fusion), channel_id=1, source_target_pairs={{0,2},{1,3},{2,0},{3,1},{4,6},{5,7},{6,4},{7,5},{8,10},{9,11},{10,... | collective-permute-start | bytes 786440 | tf_op jit(solution)/shard_map/ppermute | solution.py:243

commit v5 on v4

--- a/solution.py
+++ b/solution.py
@@ -13,9 +13,9 @@
 NEAR = SIDES * QUAD
 NEAR_ORDER = ((1, 1), (1, 2), (0, 1), (0, 2), (1, 0), (1, 3), (0, 0), (0, 3))
 FAR_ORDER = (2, 3, 1, 0)
+LEAD = 2
 HALF = jnp.bfloat16
 FULL = jnp.float32
-SMEM = pl.BlockSpec(memory_space=pltpu.SMEM)
 VMEM = pl.BlockSpec(memory_space=pltpu.VMEM)
 ANY = pl.BlockSpec(memory_space=pl.ANY)
 
@@ -48,8 +48,10 @@
     me = lax.axis_index("fsdp")
     place, y = me % QUAD, me // QUAD
     block = features.shape[1] // (COLUMN * QUAD)
-    row = lax.broadcasted_iota(jnp.int32, cotangent.shape, 0)
-    masked = jnp.where(row < lengths[0, me], cotangent[...], jnp.zeros((), cotangent.dtype))
+    mine = lax.broadcasted_iota(jnp.int32, lengths.shape, 1) == me
+    own = jnp.sum(jnp.where(mine, lengths[...].astype(FULL), 0.0), axis=1, keepdims=True)
+    row = lax.broadcasted_iota(jnp.int32, cotangent.shape, 0).astype(FULL)
+    masked = jnp.where(row < own, cotangent[...], jnp.zeros((), cotangent.dtype))
     for d in range(COLUMN):
         target = (y + d) % COLUMN
         for step in range(QUAD):
@@ -102,7 +104,7 @@
         product = (product * factor).astype(HALF)
         for d in range(COLUMN):
             part = product[d * tokens : (d + 1) * tokens]
-            results[(y + COLUMN - d) % COLUMN, :, step * block : (step + 1) * block] = part
+            results[(y + 2 * COLUMN - d - LEAD) % COLUMN, :, step * block : (step + 1) * block] = part
 
 
 def weight_kernel(*refs):
@@ -130,7 +132,7 @@
     copies = []
     for d in range(COLUMN):
         for step in range(QUAD):
-            target = (d * QUAD + block_of(place, step)) * block
+            target = ((d + LEAD) % COLUMN * QUAD + block_of(place, step)) * block
             copies.append(
                 pltpu.make_async_copy(
                     pieces.at[d, :, pl.ds(step * block, block)],
@@ -178,7 +180,7 @@
     beside = [(f, f ^ 2) for f in range(shards)]
     across = [(f, f ^ 1) for f in range(shards)]
     up = [[(f, (f + QUAD * d) % shards) for f in range(shards)] for d in range(COLUMN)]
-    columns = [[QUAD * y + j for y in range(COLUMN)] for j in range(QUAD)]
+    columns = [[QUAD * ((y + LEAD) % COLUMN) + j for y in range(COLUMN)] for j in range(QUAD)]
     depth = replicas // SIDES
     outer = depth // QUAD
     near = [[depth * h + QUAD * a + b for h, b in NEAR_ORDER] for a in range(outer)]
@@ -191,7 +193,7 @@
         pack_kernel,
         [((tokens, wide + keys), HALF)] * COLUMN,
         (lengths, activations[0], cotangent[0], pieces),
-        [SMEM, VMEM, VMEM, ANY],
+        [VMEM, VMEM, VMEM, ANY],
         moved=3 << 20,
     )
     packed = [packed[0]] + [lax.ppermute(packed[d], "fsdp", up[d]) for d in (1, 2, 3)]
@@ -241,7 +243,9 @@
     )
     crossed = lax.ppermute(sent, "fsdp", across)
     passed = lax.ppermute((grad_passed + crossed[rows:].astype(FULL)).astype(HALF), "fsdp", beside)
-    summed = grad_own + crossed[:rows].astype(FULL) + passed.astype(FULL)
+    summed = lax.optimization_barrier(grad_own + crossed[:rows].astype(FULL))
+    passed = lax.optimization_barrier((passed, spread))[0]
+    summed = summed + passed.astype(FULL)
 
     grad = summed * factor
     first = 0.9 * moment_one[0] + 0.1 * grad

time: 85.3 us -> 83.4 us (0.978)
  waiting for transfers between devices: 14.4 us -> 13.1 us
  other arithmetic: 3.2 us -> 2.21 us
  starting transfers between devices: 55.6 us -> 56.5 us
    all_to_all x1, starting transfers between devices: 3.53 us -> 4.76 us  [local(): back = lax.all_to_all(outgoing, 'fsdp', 0, 0, axis_index_groups=columns)]
    broadcast_in_dim x1, other arithmetic: 2.27 us -> 1.2 us  [local(): master_out[None]]
    unnamed x18 -> x20, local copies, waits for them, and re-layouts: 1.8 us -> 1.92 us
  transfers between devices with their start and end apart: 11 -> 11, of which waited for: 4 -> 4; matrix products, arithmetic and copies ran while one was open for 4% -> 3% of each run, Pallas kernels for 8% -> 8%
where the time goes in v5:
time: 83.4 us; the launch traced here: 82.6 us
  starting transfers between devices  56.5 us (68%)
  waiting for transfers between devices  13.1 us (16%)
  Pallas kernels  8.09 us (10%)
  other arithmetic  2.21 us (3%)
  local copies, waits for them, and re-layouts  1.92 us (2%)
    all_to_all x1, starting transfers between devices, local(): sums = lax.all_to_all(sums, 'replica', 0, 0, axis_index_groups=far)  14.4 us
    ppermute x3, starting transfers between devices, local(): lax.ppermute(packed[d], 'fsdp', up[d])  10.3 us
    all_to_all x1, starting transfers between devices, local(): lax.all_to_all(pieces, 'replica', 0, 0, axis_index_groups=near)  9.32 us
    pallas_call x8, Pallas kernels, call(): pl.pallas_call(kernel, grid=grid, out_shape=outs, in_specs=in_specs or [V...  8.09 us
    ppermute x1, waiting for transfers between devices, local(): lax.ppermute((grad_passed + crossed[rows:].astype(FULL)).astype(HALF), 'f...  6.36 us
    all_to_all x1, starting transfers between devices, local(): spread = lax.all_to_all(fresh, 'replica', 0, 0, axis_index_groups=near)  5.14 us
    all_to_all x1, starting transfers between devices, local(): back = lax.all_to_all(outgoing, 'fsdp', 0, 0, axis_index_groups=columns)  4.76 us
    ppermute x1, starting transfers between devices, local(): both = lax.ppermute(jnp.concatenate([own, other], axis=0), 'fsdp', across)  4.36 us
  transfers between devices with their start and end apart: 11, of which 4 were waited for; matrix products, arithmetic and copies ran while one was open for 3% of the time, Pallas kernels for 8%

profile of v5, /device:TPU:1, one launch (start us, length us, event | category | flops | bytes accessed | tf_op | source)
XLA Modules:
  0.0 82.6 jit_solution(4176717363252564872)
XLA Ops:
  0.7 1.1 %copy-done.1 = f32[1,1,256,512]{3,2,1,0:T(8,128)S(1)} copy-done((f32[1,1,256,512]{3,2,1,0:T(8,128)S(1)}, f32[1,1,256,512]{3,2,1,0:T(8,128)}, u32[]{:S(2)}) %copy-start.1) | copy-done | bytes 524312
  1.8 0.7 shard_map.128.after
  2.5 9.3 %all-to-all-start = ((bf16[8,32,512]{2,1,0:T(8,128)(2,1)}), bf16[8,32,512]{2,1,0:T(8,128)(2,1)S(1)}, u32[]{:S(2)}, u32[]{:S(2)}) async-start(bf16[8,32,512]{2,1,0:T(8,128)(2,1)} %shard_map.128.after), calls=%async_computation | async-start | bytes 524288 | tf_op jit(solution)/shard_map/all_to_all | solution.py:190
  12.5 0.9 %shard_map.129 = (bf16[128,1536]{1,0:T(8,128)(2,1)S(1)}, bf16[128,1536]{1,0:T(8,128)(2,1)S(1)}, bf16[128,1536]{1,0:T(8,128)(2,1)}, bf16[128,1536]{1,0:T(8,128)(2,1)S(1)}) custom-call(s32[1,16]{1,0:T(1,128)S(1)} %copy-done.5, bf16[128,4096]{1,0:T(8,128)(2,1)S(1)} %bitcast.31, bf16[128,512]{1,0:T(8,128)(2,1)S(1)} %bitcast.33, bf16[8,32,512]{2,1,0:T(8,128)(2,1)} %shard_map.128.after), custom_call_target="tpu_custom_call" | custom-call | bytes 3145728 | tf_op jit(solution)/shard_map/pallas_call | solution.py:155
  13.6 3.1 %collective-permute-start = (bf16[256,512]{1,0:T(8,128)(2,1)S(1)}, bf16[256,512]{1,0:T(8,128)(2,1)S(1)}, u32[]{:S(2)}, u32[]{:S(2)}) collective-permute-start(bf16[256,512]{1,0:T(8,128)(2,1)S(1)} %convert_element_type.15.refs_1_), channel_id=1, source_target_pairs={{0,2},{1,3},{2,0},{3,1},{4,6},{5,7},{6,4},{7,5},{8,10},{9,11},{10,... | collective-permute-start | bytes 786440 | tf_op jit(solution)/shard_map/ppermute | solution.py:203
  16.6 4.8 %collective-permute-start.1 = (bf16[128,1536]{1,0:T(8,128)(2,1)}, bf16[128,1536]{1,0:T(8,128)(2,1)S(1)}, u32[]{:S(2)}, u32[]{:S(2)}) collective-permute-start(bf16[128,1536]{1,0:T(8,128)(2,1)} %get-tuple-element.23), channel_id=1, source_target_pairs={{0,8},{1,9},{2,10},{3,11},{4,12},{5,13},{6,14},{7,15},{8,0},{9,1},... | collective-permute-start | bytes 1179656 | tf_op jit(solution)/shard_map/ppermute | solution.py:199
  21.5 2.7 %collective-permute-start.2 = (bf16[128,1536]{1,0:T(8,128)(2,1)S(1)}, bf16[128,1536]{1,0:T(8,128)(2,1)S(1)}, u32[]{:S(2)}, u32[]{:S(2)}) collective-permute-start(bf16[128,1536]{1,0:T(8,128)(2,1)S(1)} %get-tuple-element.24), channel_id=1, source_target_pairs={{0,12},{1,13},{2,14},{3,15},{4,0},{5,1},{6,2},{7,3},{8,4},{9,5},{1... | collective-permute-start | bytes 1179656 | tf_op jit(solution)/shard_map/ppermute | solution.py:199
  24.9 14.4 %all-to-all-start.1 = ((bf16[4,48,512]{2,1,0:T(8,128)(2,1)}), bf16[4,48,512]{2,1,0:T(8,128)(2,1)S(1)}, u32[]{:S(2)}, u32[]{:S(2)}) async-start(bf16[4,48,512]{2,1,0:T(8,128)(2,1)} %shard_map.130), calls=%async_computation.1 | async-start | bytes 393216 | tf_op jit(solution)/shard_map/all_to_all | solution.py:213
  39.3 0.8 %pad_maximum_fusion = bf16[512,512]{1,0:T(8,128)(2,1)} fusion(bf16[256,512]{1,0:T(8,128)(2,1)S(1)} %collective-permute-done.later.refs_2_, bf16[256,512]{1,0:T(8,128)(2,1)S(1)} %convert_element_type.15.refs_1_), kind=kLoop, calls=%fused_computation | loop fusion | flops 1048576 | bytes 1048576 | tf_op jit(solution)/shard_map/concatenate | solution.py:212
  40.1 4.4 %collective-permute-start.3 = (bf16[512,512]{1,0:T(8,128)(2,1)}, bf16[512,512]{1,0:T(8,128)(2,1)S(1)}, u32[]{:S(2)}, u32[]{:S(2)}) collective-permute-start(bf16[512,512]{1,0:T(8,128)(2,1)} %pad_maximum_fusion), channel_id=1, source_target_pairs={{0,1},{1,0},{2,3},{3,2},{4,5},{5,4},{6,7},{7,6},{8,9},{9,8},{10,11... | collective-permute-start | bytes 1572872 | tf_op jit(solution)/shard_map/ppermute | solution.py:212
  44.5 2.8 %collective-permute-start.4 = (bf16[128,1536]{1,0:T(8,128)(2,1)S(1)}, bf16[128,1536]{1,0:T(8,128)(2,1)S(1)}, u32[]{:S(2)}, u32[]{:S(2)}) collective-permute-start(bf16[128,1536]{1,0:T(8,128)(2,1)S(1)} %get-tuple-element.26), channel_id=1, source_target_pairs={{0,4},{1,5},{2,6},{3,7},{4,8},{5,9},{6,10},{7,11},{8,12},{9,13},{1... | collective-permute-start | bytes 1179656 | tf_op jit(solution)/shard_map/ppermute | solution.py:199
  47.3 1.7 %all-to-all-done.1.sums = bf16[4,48,512]{2,1,0:T(8,128)(2,1)S(1)} async-done(((bf16[4,48,512]{2,1,0:T(8,128)(2,1)}), bf16[4,48,512]{2,1,0:T(8,128)(2,1)S(1)}, u32[]{:S(2)}, u32[]{:S(2)}) %all-to-all-start.1) | async-done | bytes 196640 | tf_op jit(solution)/shard_map/all_to_all | solution.py:213
  49.0 0.8 shard_map.131
  49.7 5.1 %all-to-all-start.2 = ((bf16[8,32,512]{2,1,0:T(8,128)(2,1)}), bf16[8,32,512]{2,1,0:T(8,128)(2,1)S(1)}, u32[]{:S(2)}, u32[]{:S(2)}) async-start(bf16[8,32,512]{2,1,0:T(8,128)(2,1)} %get-tuple-element.22.refs_0_), calls=%async_computation.2 | async-start | bytes 524288 | tf_op jit(solution)/shard_map/all_to_all | solution.py:231
  54.9 3.5 %collective-permute-done.4.refs_5_.refs_1_ = bf16[128,1536]{1,0:T(8,128)(2,1)S(1)} collective-permute-done((bf16[128,1536]{1,0:T(8,128)(2,1)S(1)}, bf16[128,1536]{1,0:T(8,128)(2,1)S(1)}, u32[]{:S(2)}, u32[]{:S(2)}) %collective-permute-start.4) | collective-permute-done | bytes 393248 | tf_op jit(solution)/shard_map/ppermute | solution.py:199
  58.3 1.8 %shard_map.132.refs_4_ = bf16[4,128,1024]{2,1,0:T(8,128)(2,1)} custom-call(bf16[8,32,512]{2,1,0:T(8,128)(2,1)} %get-tuple-element.22.refs_0_, bf16[256,512]{1,0:T(8,128)(2,1)S(1)} %convert_element_type.15.refs_1_, bf16[256,512]{1,0:T(8,128)(2,1)S(1)} %collective-permute-done.later.refs_2_, bf16[512,512]{1,0:T(8,128)(2,1)S(1)} %collective-permute-done.3.refs_3_, ...), custom_call_target="tpu_custom_call" | custom-call | flops 536870912 | bytes 3145728 | tf_op jit(solution)/shard_map/pallas_call | solution.py:155
  60.1 1.4 %shard_map.134 = (f32[256,512]{1,0:T(8,128)S(1)}, f32[256,512]{1,0:T(8,128)S(1)}, bf16[512,512]{1,0:T(8,128)(2,1)}) custom-call(bf16[128,1536]{1,0:T(8,128)(2,1)S(1)} %get-tuple-element.20.after.refs_4_.refs_0_, bf16[128,1536]{1,0:T(8,128)(2,1)S(1)} %collective-permute-done.4.refs_5_.refs_1_, bf16[128,1536]{1,0:T(8,128)(2,1)S(1)} %collective-permute-done.1.refs_6_.refs_2_, ...), custom_call_target="tpu_custom_call" | custom-call | flops 536870912 | bytes 5242880 | tf_op jit(solution)/shard_map/pallas_call | solution.py:155
  61.5 2.7 %collective-permute-start.5 = (bf16[512,512]{1,0:T(8,128)(2,1)}, bf16[512,512]{1,0:T(8,128)(2,1)S(1)}, u32[]{:S(2)}, u32[]{:S(2)}) collective-permute-start(bf16[512,512]{1,0:T(8,128)(2,1)} %get-tuple-element.29), channel_id=1, source_target_pairs={{0,1},{1,0},{2,3},{3,2},{4,5},{5,4},{6,7},{7,6},{8,9},{9,8},{10,11... | collective-permute-start | bytes 1572872 | tf_op jit(solution)/shard_map/ppermute | solution.py:244
  64.2 4.8 %all-to-all-start.3 = ((bf16[4,128,1024]{2,1,0:T(8,128)(2,1)}), bf16[4,128,1024]{2,1,0:T(8,128)(2,1)S(1)}, u32[]{:S(2)}, u32[]{:S(2)}) async-start(bf16[4,128,1024]{2,1,0:T(8,128)(2,1)} %shard_map.132.refs_4_), calls=%async_computation.3 | async-start | bytes 2097152 | tf_op jit(solution)/shard_map/all_to_all | solution.py:233
  69.2 2.5 %collective-permute-start.6 = (bf16[256,512]{1,0:T(8,128)(2,1)S(1)}, bf16[256,512]{1,0:T(8,128)(2,1)S(1)}, u32[]{:S(2)}, u32[]{:S(2)}) collective-permute-start(bf16[256,512]{1,0:T(8,128)(2,1)S(1)} %get-tuple-element.35), channel_id=1, source_target_pairs={{0,2},{1,3},{2,0},{3,1},{4,6},{5,7},{6,4},{7,5},{8,10},{9,11},{10,... | collective-permute-start | bytes 786440 | tf_op jit(solution)/shard_map/ppermute | solution.py:245
  72.4 6.4 %collective-permute-done.6 = bf16[256,512]{1,0:T(8,128)(2,1)S(1)} collective-permute-done((bf16[256,512]{1,0:T(8,128)(2,1)S(1)}, bf16[256,512]{1,0:T(8,128)(2,1)S(1)}, u32[]{:S(2)}, u32[]{:S(2)}) %collective-permute-start.6) | collective-permute-done | bytes 262176 | tf_op jit(solution)/shard_map/ppermute | solution.py:245
  78.8 1.2 %fusion.4 = f32[1,256,512]{2,1,0:T(8,128)} fusion(f32[1,256,512]{2,1,0:T(8,128)S(1)} %copy-done.8, f32[256,512]{1,0:T(8,128)S(1)} %get-tuple-element.36, bf16[256,512]{1,0:T(8,128)(2,1)S(1)} %collective-permute-done.6, f32[1,256,512]{2,1,0:T(8,128)S(1)} %copy-done.9, f32[1,256,512]{2,1,0:T(8,128)S(1)} %copy-done.7), kind=kLoop, calls=%fused_computation.6 | loop fusion | flops 1966080 | bytes 2883584 | tf_op jit(solution)/shard_map/broadcast_in_dim | solution.py:265
  80.0 1.5 %all-to-all-done.3.refs_0_ = bf16[4,128,1024]{2,1,0:T(8,128)(2,1)S(1)} async-done(((bf16[4,128,1024]{2,1,0:T(8,128)(2,1)}), bf16[4,128,1024]{2,1,0:T(8,128)(2,1)S(1)}, u32[]{:S(2)}, u32[]{:S(2)}) %all-to-all-start.3) | async-done | bytes 1048608 | tf_op jit(solution)/shard_map/all_to_all | solution.py:233
  81.5 1.1 %shard_map.133 = bf16[128,4096]{1,0:T(8,128)(2,1)} custom-call(bf16[4,128,1024]{2,1,0:T(8,128)(2,1)S(1)} %all-to-all-done.3.refs_0_), custom_call_target="tpu_custom_call" | custom-call | bytes 2097152 | tf_op jit(solution)/shard_map/pallas_call | solution.py:155
  (30 shorter events, 2.4 us)
Async XLA Ops:
  0.6 11.2 %copy-start = (bf16[1,128,4096]{2,1,0:T(8,128)(2,1)S(1)}, bf16[1,128,4096]{2,1,0:T(8,128)(2,1)}, u32[]{:S(2)}) copy-start(bf16[1,128,4096]{2,1,0:T(8,128)(2,1)} %param.9) | copy-start | bytes 3145732
  0.6 1.1 %copy-start.1 = (f32[1,1,256,512]{3,2,1,0:T(8,128)S(1)}, f32[1,1,256,512]{3,2,1,0:T(8,128)}, u32[]{:S(2)}) copy-start(f32[1,1,256,512]{3,2,1,0:T(8,128)} %param.15) | copy-start | bytes 1572868
  2.5 9.3 %copy-start.2 = (bf16[1,128,512]{2,1,0:T(8,128)(2,1)S(1)}, bf16[1,128,512]{2,1,0:T(8,128)(2,1)}, u32[]{:S(2)}) copy-start(bf16[1,128,512]{2,1,0:T(8,128)(2,1)} %param.10) | copy-start | bytes 393220
  2.5 21.7 %all-to-all-start = ((bf16[8,32,512]{2,1,0:T(8,128)(2,1)}), bf16[8,32,512]{2,1,0:T(8,128)(2,1)S(1)}, u32[]{:S(2)}, u32[]{:S(2)}) async-start(bf16[8,32,512]{2,1,0:T(8,128)(2,1)} %shard_map.128.after), calls=%async_computation | async-start | bytes 524288 | tf_op jit(solution)/shard_map/all_to_all | solution.py:190
  11.8 0.7 copy-start.5
  12.5 1.0 %copy-start.6 = (f32[1,256,512]{2,1,0:T(8,128)S(1)}, f32[1,256,512]{2,1,0:T(8,128)}, u32[]{:S(2)}) copy-start(f32[1,256,512]{2,1,0:T(8,128)} %param.11) | copy-start | bytes 1572868
  13.5 10.7 %copy-start.3 = (f32[1,8,512]{2,1,0:T(8,128)S(1)}, f32[1,8,512]{2,1,0:T(8,128)}, u32[]{:S(2)}) copy-start(f32[1,8,512]{2,1,0:T(8,128)} %param.16) | copy-start | bytes 49156
  13.5 10.7 %copy-start.4 = (f32[1,8,512]{2,1,0:T(8,128)S(1)}, f32[1,8,512]{2,1,0:T(8,128)}, u32[]{:S(2)}) copy-start(f32[1,8,512]{2,1,0:T(8,128)} %param.17) | copy-start | bytes 49156
  13.6 10.6 %collective-permute-start = (bf16[256,512]{1,0:T(8,128)(2,1)S(1)}, bf16[256,512]{1,0:T(8,128)(2,1)S(1)}, u32[]{:S(2)}, u32[]{:S(2)}) collective-permute-start(bf16[256,512]{1,0:T(8,128)(2,1)S(1)} %convert_element_type.15.refs_1_), channel_id=1, source_target_pairs={{0,2},{1,3},{2,0},{3,1},{4,6},{5,7},{6,4},{7,5},{8,10},{9,11},{10,... | collective-permute-start | bytes 786440 | tf_op jit(solution)/shard_map/ppermute | solution.py:203
  16.6 22.7 %collective-permute-start.1 = (bf16[128,1536]{1,0:T(8,128)(2,1)}, bf16[128,1536]{1,0:T(8,128)(2,1)S(1)}, u32[]{:S(2)}, u32[]{:S(2)}) collective-permute-start(bf16[128,1536]{1,0:T(8,128)(2,1)} %get-tuple-element.23), channel_id=1, source_target_pairs={{0,8},{1,9},{2,10},{3,11},{4,12},{5,13},{6,14},{7,15},{8,0},{9,1},... | collective-permute-start | bytes 1179656 | tf_op jit(solution)/shard_map/ppermute | solution.py:199
  21.5 17.8 %collective-permute-start.2 = (bf16[128,1536]{1,0:T(8,128)(2,1)S(1)}, bf16[128,1536]{1,0:T(8,128)(2,1)S(1)}, u32[]{:S(2)}, u32[]{:S(2)}) collective-permute-start(bf16[128,1536]{1,0:T(8,128)(2,1)S(1)} %get-tuple-element.24), channel_id=1, source_target_pairs={{0,12},{1,13},{2,14},{3,15},{4,0},{5,1},{6,2},{7,3},{8,4},{9,5},{1... | collective-permute-start | bytes 1179656 | tf_op jit(solution)/shard_map/ppermute | solution.py:199
  24.9 24.0 %all-to-all-start.1 = ((bf16[4,48,512]{2,1,0:T(8,128)(2,1)}), bf16[4,48,512]{2,1,0:T(8,128)(2,1)S(1)}, u32[]{:S(2)}, u32[]{:S(2)}) async-start(bf16[4,48,512]{2,1,0:T(8,128)(2,1)} %shard_map.130), calls=%async_computation.1 | async-start | bytes 393216 | tf_op jit(solution)/shard_map/all_to_all | solution.py:213
  40.1 18.2 %collective-permute-start.3 = (bf16[512,512]{1,0:T(8,128)(2,1)}, bf16[512,512]{1,0:T(8,128)(2,1)S(1)}, u32[]{:S(2)}, u32[]{:S(2)}) collective-permute-start(bf16[512,512]{1,0:T(8,128)(2,1)} %pad_maximum_fusion), channel_id=1, source_target_pairs={{0,1},{1,0},{2,3},{3,2},{4,5},{5,4},{6,7},{7,6},{8,9},{9,8},{10,11... | collective-permute-start | bytes 1572872 | tf_op jit(solution)/shard_map/ppermute | solution.py:212
  44.5 13.8 %collective-permute-start.4 = (bf16[128,1536]{1,0:T(8,128)(2,1)S(1)}, bf16[128,1536]{1,0:T(8,128)(2,1)S(1)}, u32[]{:S(2)}, u32[]{:S(2)}) collective-permute-start(bf16[128,1536]{1,0:T(8,128)(2,1)S(1)} %get-tuple-element.26), channel_id=1, source_target_pairs={{0,4},{1,5},{2,6},{3,7},{4,8},{5,9},{6,10},{7,11},{8,12},{9,13},{1... | collective-permute-start | bytes 1179656 | tf_op jit(solution)/shard_map/ppermute | solution.py:199
  49.7 14.5 %all-to-all-start.2 = ((bf16[8,32,512]{2,1,0:T(8,128)(2,1)}), bf16[8,32,512]{2,1,0:T(8,128)(2,1)S(1)}, u32[]{:S(2)}, u32[]{:S(2)}) async-start(bf16[8,32,512]{2,1,0:T(8,128)(2,1)} %get-tuple-element.22.refs_0_), calls=%async_computation.2 | async-start | bytes 524288 | tf_op jit(solution)/shard_map/all_to_all | solution.py:231
  61.5 7.5 %collective-permute-start.5 = (bf16[512,512]{1,0:T(8,128)(2,1)}, bf16[512,512]{1,0:T(8,128)(2,1)S(1)}, u32[]{:S(2)}, u32[]{:S(2)}) collective-permute-start(bf16[512,512]{1,0:T(8,128)(2,1)} %get-tuple-element.29), channel_id=1, source_target_pairs={{0,1},{1,0},{2,3},{3,2},{4,5},{5,4},{6,7},{7,6},{8,9},{9,8},{10,11... | collective-permute-start | bytes 1572872 | tf_op jit(solution)/shard_map/ppermute | solution.py:244
  64.2 17.3 %all-to-all-start.3 = ((bf16[4,128,1024]{2,1,0:T(8,128)(2,1)}), bf16[4,128,1024]{2,1,0:T(8,128)(2,1)S(1)}, u32[]{:S(2)}, u32[]{:S(2)}) async-start(bf16[4,128,1024]{2,1,0:T(8,128)(2,1)} %shard_map.132.refs_4_), calls=%async_computation.3 | async-start | bytes 2097152 | tf_op jit(solution)/shard_map/all_to_all | solution.py:233
  69.0 9.8 %copy-start.8 = (f32[1,256,512]{2,1,0:T(8,128)S(1)}, f32[1,256,512]{2,1,0:T(8,128)}, u32[]{:S(2)}) copy-start(f32[1,256,512]{2,1,0:T(8,128)} %param.13) | copy-start | bytes 1572868
  69.0 9.8 %copy-start.9 = (f32[1,256,512]{2,1,0:T(8,128)S(1)}, f32[1,256,512]{2,1,0:T(8,128)}, u32[]{:S(2)}) copy-start(f32[1,256,512]{2,1,0:T(8,128)} %param.12) | copy-start | bytes 1572868
  69.1 9.7 %copy-start.7 = (f32[1,256,512]{2,1,0:T(8,128)S(1)}, f32[1,256,512]{2,1,0:T(8,128)}, u32[]{:S(2)}) copy-start(f32[1,256,512]{2,1,0:T(8,128)} %param.11) | copy-start | bytes 1572868
  69.2 9.6 %collective-permute-start.6 = (bf16[256,512]{1,0:T(8,128)(2,1)S(1)}, bf16[256,512]{1,0:T(8,128)(2,1)S(1)}, u32[]{:S(2)}, u32[]{:S(2)}) collective-permute-start(bf16[256,512]{1,0:T(8,128)(2,1)S(1)} %get-tuple-element.35), channel_id=1, source_target_pairs={{0,2},{1,3},{2,0},{3,1},{4,6},{5,7},{6,4},{7,5},{8,10},{9,11},{10,... | collective-permute-start | bytes 786440 | tf_op jit(solution)/shard_map/ppermute | solution.py:245

commit v6 on v5

--- a/solution.py
+++ b/solution.py
@@ -11,7 +11,7 @@
 COLUMN = 4
 SIDES = 2
 NEAR = SIDES * QUAD
-NEAR_ORDER = ((1, 1), (1, 2), (0, 1), (0, 2), (1, 0), (1, 3), (0, 0), (0, 3))
+NEAR_ORDER = ((1, 2), (1, 1), (0, 2), (0, 1), (1, 3), (1, 0), (0, 3), (0, 0))
 FAR_ORDER = (2, 3, 1, 0)
 LEAD = 2
 HALF = jnp.bfloat16
@@ -208,7 +208,7 @@
         (near_pieces, anchor[0], momentum[0], packed[0], other),
         [VMEM, VMEM, VMEM, ANY, ANY],
     )
-    other = lax.optimization_barrier((other, sums, packed[2], packed[3]))[0]
+    other = lax.optimization_barrier((other, sums, packed[1], packed[2], packed[3]))[0]
     both = lax.ppermute(jnp.concatenate([own, other], axis=0), "fsdp", across)
     sums = lax.all_to_all(sums, "replica", 0, 0, axis_index_groups=far)
     anchor_out, momentum_out, fresh = call(

time: 83.4 us -> 84.7 us (1.016)
  starting transfers between devices: 56.5 us -> 60.4 us
  waiting for transfers between devices: 13.1 us -> 11.3 us
    ppermute x3, waiting for transfers between devices: 3.49 us -> 0.01 us  [local(): lax.ppermute(packed[d], 'fsdp', up[d])]
    ppermute x1, starting transfers between devices: 2.69 us -> 4.86 us  [local(): crossed = lax.ppermute(sent, 'fsdp', across)]
    all_to_all x1, waiting for transfers between devices: 1.69 us -> 3.75 us  [local(): sums = lax.all_to_all(sums, 'replica', 0, 0, axis_index_groups=far)]
    all_to_all x1, starting transfers between devices: 5.14 us -> 6.04 us  [local(): spread = lax.all_to_all(fresh, 'replica', 0, 0, axis_index_groups=near)]
  transfers between devices with their start and end apart: 11 -> 11, of which waited for: 4 -> 3; matrix products, arithmetic and copies ran while one was open for 3% -> 2% of each run, Pallas kernels for 8% -> 7%
where the time goes in v6:
time: 84.7 us; the launch traced here: 83.9 us
  starting transfers between devices  60.4 us (71%)
  waiting for transfers between devices  11.3 us (13%)
  Pallas kernels  8.1 us (10%)
  local copies, waits for them, and re-layouts  1.92 us (2%)
  other arithmetic  1.42 us (2%)
    all_to_all x1, starting transfers between devices, local(): sums = lax.all_to_all(sums, 'replica', 0, 0, axis_index_groups=far)  14.7 us
    ppermute x3, starting transfers between devices, local(): lax.ppermute(packed[d], 'fsdp', up[d])  10.7 us
    all_to_all x1, starting transfers between devices, local(): lax.all_to_all(pieces, 'replica', 0, 0, axis_index_groups=near)  9.77 us
    pallas_call x8, Pallas kernels, call(): pl.pallas_call(kernel, grid=grid, out_shape=outs, in_specs=in_specs or [V...  8.1 us
    all_to_all x1, starting transfers between devices, local(): spread = lax.all_to_all(fresh, 'replica', 0, 0, axis_index_groups=near)  6.04 us
    ppermute x1, waiting for transfers between devices, local(): lax.ppermute((grad_passed + crossed[rows:].astype(FULL)).astype(HALF), 'f...  5.86 us
    ppermute x1, starting transfers between devices, local(): crossed = lax.ppermute(sent, 'fsdp', across)  4.86 us
    ppermute x1, starting transfers between devices, local(): both = lax.ppermute(jnp.concatenate([own, other], axis=0), 'fsdp', across)  4.76 us
  transfers between devices with their start and end apart: 11, of which 3 were waited for; matrix products, arithmetic and copies ran while one was open for 2% of the time, Pallas kernels for 7%

profile of v6, /device:TPU:1, one launch (start us, length us, event | category | flops | bytes accessed | tf_op | source)
XLA Modules:
  0.0 83.9 jit_solution(14509583070802547590)
XLA Ops:
  0.7 1.1 %copy-done.1 = f32[1,1,256,512]{3,2,1,0:T(8,128)S(1)} copy-done((f32[1,1,256,512]{3,2,1,0:T(8,128)S(1)}, f32[1,1,256,512]{3,2,1,0:T(8,128)}, u32[]{:S(2)}) %copy-start.1) | copy-done | bytes 524312
  1.8 0.7 shard_map.128.after
  2.5 9.8 %all-to-all-start = ((bf16[8,32,512]{2,1,0:T(8,128)(2,1)}), bf16[8,32,512]{2,1,0:T(8,128)(2,1)S(1)}, u32[]{:S(2)}, u32[]{:S(2)}) async-start(bf16[8,32,512]{2,1,0:T(8,128)(2,1)} %shard_map.128.after), calls=%async_computation | async-start | bytes 524288 | tf_op jit(solution)/shard_map/all_to_all | solution.py:190
  12.9 0.9 %shard_map.129 = (bf16[128,1536]{1,0:T(8,128)(2,1)S(1)}, bf16[128,1536]{1,0:T(8,128)(2,1)}, bf16[128,1536]{1,0:T(8,128)(2,1)S(1)}, bf16[128,1536]{1,0:T(8,128)(2,1)S(1)}) custom-call(s32[1,16]{1,0:T(1,128)S(1)} %copy-done.5, bf16[128,4096]{1,0:T(8,128)(2,1)S(1)} %bitcast.31, bf16[128,512]{1,0:T(8,128)(2,1)S(1)} %bitcast.33, bf16[8,32,512]{2,1,0:T(8,128)(2,1)} %shard_map.128.after), custom_call_target="tpu_custom_call" | custom-call | bytes 3145728 | tf_op jit(solution)/shard_map/pallas_call | solution.py:155
  14.0 2.6 %collective-permute-start = (bf16[256,512]{1,0:T(8,128)(2,1)S(1)}, bf16[256,512]{1,0:T(8,128)(2,1)S(1)}, u32[]{:S(2)}, u32[]{:S(2)}) collective-permute-start(bf16[256,512]{1,0:T(8,128)(2,1)S(1)} %convert_element_type.15.refs_1_), channel_id=1, source_target_pairs={{0,2},{1,3},{2,0},{3,1},{4,6},{5,7},{6,4},{7,5},{8,10},{9,11},{10,... | collective-permute-start | bytes 786440 | tf_op jit(solution)/shard_map/ppermute | solution.py:203
  16.6 3.2 %collective-permute-start.1 = (bf16[128,1536]{1,0:T(8,128)(2,1)}, bf16[128,1536]{1,0:T(8,128)(2,1)S(1)}, u32[]{:S(2)}, u32[]{:S(2)}) collective-permute-start(bf16[128,1536]{1,0:T(8,128)(2,1)} %get-tuple-element.23), channel_id=1, source_target_pairs={{0,4},{1,5},{2,6},{3,7},{4,8},{5,9},{6,10},{7,11},{8,12},{9,13},{1... | collective-permute-start | bytes 1179656 | tf_op jit(solution)/shard_map/ppermute | solution.py:199
  19.8 4.5 %collective-permute-start.2 = (bf16[128,1536]{1,0:T(8,128)(2,1)S(1)}, bf16[128,1536]{1,0:T(8,128)(2,1)S(1)}, u32[]{:S(2)}, u32[]{:S(2)}) collective-permute-start(bf16[128,1536]{1,0:T(8,128)(2,1)S(1)} %get-tuple-element.24), channel_id=1, source_target_pairs={{0,8},{1,9},{2,10},{3,11},{4,12},{5,13},{6,14},{7,15},{8,0},{9,1},... | collective-permute-start | bytes 1179656 | tf_op jit(solution)/shard_map/ppermute | solution.py:199
  24.4 3.0 %collective-permute-start.3 = (bf16[128,1536]{1,0:T(8,128)(2,1)S(1)}, bf16[128,1536]{1,0:T(8,128)(2,1)S(1)}, u32[]{:S(2)}, u32[]{:S(2)}) collective-permute-start(bf16[128,1536]{1,0:T(8,128)(2,1)S(1)} %get-tuple-element.25), channel_id=1, source_target_pairs={{0,12},{1,13},{2,14},{3,15},{4,0},{5,1},{6,2},{7,3},{8,4},{9,5},{1... | collective-permute-start | bytes 1179656 | tf_op jit(solution)/shard_map/ppermute | solution.py:199
  27.4 0.7 shard_map.130
  28.1 14.7 %all-to-all-start.1 = ((bf16[4,48,512]{2,1,0:T(8,128)(2,1)}), bf16[4,48,512]{2,1,0:T(8,128)(2,1)S(1)}, u32[]{:S(2)}, u32[]{:S(2)}) async-start(bf16[4,48,512]{2,1,0:T(8,128)(2,1)} %shard_map.130), calls=%async_computation.1 | async-start | bytes 393216 | tf_op jit(solution)/shard_map/all_to_all | solution.py:213
  42.9 4.8 %collective-permute-start.4 = (bf16[512,512]{1,0:T(8,128)(2,1)S(1)}, bf16[512,512]{1,0:T(8,128)(2,1)S(1)}, u32[]{:S(2)}, u32[]{:S(2)}) collective-permute-start(bf16[512,512]{1,0:T(8,128)(2,1)S(1)} %pad_maximum_fusion), channel_id=1, source_target_pairs={{0,1},{1,0},{2,3},{3,2},{4,5},{5,4},{6,7},{7,6},{8,9},{9,8},{10,11... | collective-permute-start | bytes 1572872 | tf_op jit(solution)/shard_map/ppermute | solution.py:212
  47.7 3.7 %all-to-all-done.1.sums = bf16[4,48,512]{2,1,0:T(8,128)(2,1)S(1)} async-done(((bf16[4,48,512]{2,1,0:T(8,128)(2,1)}), bf16[4,48,512]{2,1,0:T(8,128)(2,1)S(1)}, u32[]{:S(2)}, u32[]{:S(2)}) %all-to-all-start.1) | async-done | bytes 196640 | tf_op jit(solution)/shard_map/all_to_all | solution.py:213
  51.4 0.8 shard_map.131
  52.2 6.0 %all-to-all-start.2 = ((bf16[8,32,512]{2,1,0:T(8,128)(2,1)}), bf16[8,32,512]{2,1,0:T(8,128)(2,1)S(1)}, u32[]{:S(2)}, u32[]{:S(2)}) async-start(bf16[8,32,512]{2,1,0:T(8,128)(2,1)} %get-tuple-element.22.refs_0_), calls=%async_computation.2 | async-start | bytes 524288 | tf_op jit(solution)/shard_map/all_to_all | solution.py:231
  58.2 1.8 %shard_map.132.refs_4_ = bf16[4,128,1024]{2,1,0:T(8,128)(2,1)} custom-call(bf16[8,32,512]{2,1,0:T(8,128)(2,1)} %get-tuple-element.22.refs_0_, bf16[256,512]{1,0:T(8,128)(2,1)S(1)} %convert_element_type.15.refs_1_, bf16[256,512]{1,0:T(8,128)(2,1)S(1)} %collective-permute-done.later.refs_2_, bf16[512,512]{1,0:T(8,128)(2,1)S(1)} %collective-permute-done.4.refs_3_, ...), custom_call_target="tpu_custom_call" | custom-call | flops 536870912 | bytes 3145728 | tf_op jit(solution)/shard_map/pallas_call | solution.py:155
  60.0 1.4 %shard_map.134 = (f32[256,512]{1,0:T(8,128)S(1)}, f32[256,512]{1,0:T(8,128)S(1)}, bf16[512,512]{1,0:T(8,128)(2,1)}) custom-call(bf16[128,1536]{1,0:T(8,128)(2,1)S(1)} %get-tuple-element.20.after.refs_4_.refs_0_, bf16[128,1536]{1,0:T(8,128)(2,1)S(1)} %collective-permute-done.1.refs_5_.refs_1_, bf16[128,1536]{1,0:T(8,128)(2,1)S(1)} %collective-permute-done.2.refs_6_.refs_2_, ...), custom_call_target="tpu_custom_call" | custom-call | flops 536870912 | bytes 5242880 | tf_op jit(solution)/shard_map/pallas_call | solution.py:155
  61.4 4.9 %collective-permute-start.5 = (bf16[512,512]{1,0:T(8,128)(2,1)}, bf16[512,512]{1,0:T(8,128)(2,1)S(1)}, u32[]{:S(2)}, u32[]{:S(2)}) collective-permute-start(bf16[512,512]{1,0:T(8,128)(2,1)} %get-tuple-element.29), channel_id=1, source_target_pairs={{0,1},{1,0},{2,3},{3,2},{4,5},{5,4},{6,7},{7,6},{8,9},{9,8},{10,11... | collective-permute-start | bytes 1572872 | tf_op jit(solution)/shard_map/ppermute | solution.py:244
  66.3 4.2 %all-to-all-start.3 = ((bf16[4,128,1024]{2,1,0:T(8,128)(2,1)}), bf16[4,128,1024]{2,1,0:T(8,128)(2,1)S(1)}, u32[]{:S(2)}, u32[]{:S(2)}) async-start(bf16[4,128,1024]{2,1,0:T(8,128)(2,1)} %shard_map.132.refs_4_), calls=%async_computation.3 | async-start | bytes 2097152 | tf_op jit(solution)/shard_map/all_to_all | solution.py:233
  70.7 2.7 %collective-permute-start.6 = (bf16[256,512]{1,0:T(8,128)(2,1)S(1)}, bf16[256,512]{1,0:T(8,128)(2,1)S(1)}, u32[]{:S(2)}, u32[]{:S(2)}) collective-permute-start(bf16[256,512]{1,0:T(8,128)(2,1)S(1)} %get-tuple-element.35), channel_id=1, source_target_pairs={{0,2},{1,3},{2,0},{3,1},{4,6},{5,7},{6,4},{7,5},{8,10},{9,11},{10,... | collective-permute-start | bytes 786440 | tf_op jit(solution)/shard_map/ppermute | solution.py:245
  73.4 0.7 shard_map.135
  74.1 5.9 %collective-permute-done.6 = bf16[256,512]{1,0:T(8,128)(2,1)S(1)} collective-permute-done((bf16[256,512]{1,0:T(8,128)(2,1)S(1)}, bf16[256,512]{1,0:T(8,128)(2,1)S(1)}, u32[]{:S(2)}, u32[]{:S(2)}) %collective-permute-start.6) | collective-permute-done | bytes 262176 | tf_op jit(solution)/shard_map/ppermute | solution.py:245
  80.0 1.2 %fusion.4 = f32[1,256,512]{2,1,0:T(8,128)} fusion(f32[1,256,512]{2,1,0:T(8,128)S(1)} %copy-done.8, f32[256,512]{1,0:T(8,128)S(1)} %get-tuple-element.36, bf16[256,512]{1,0:T(8,128)(2,1)S(1)} %collective-permute-done.6, f32[1,256,512]{2,1,0:T(8,128)S(1)} %copy-done.9, f32[1,256,512]{2,1,0:T(8,128)S(1)} %copy-done.7), kind=kLoop, calls=%fused_computation.6 | loop fusion | flops 1966080 | bytes 2883584 | tf_op jit(solution)/shard_map/broadcast_in_dim | solution.py:265
  81.2 1.6 %all-to-all-done.3.refs_0_ = bf16[4,128,1024]{2,1,0:T(8,128)(2,1)S(1)} async-done(((bf16[4,128,1024]{2,1,0:T(8,128)(2,1)}), bf16[4,128,1024]{2,1,0:T(8,128)(2,1)S(1)}, u32[]{:S(2)}, u32[]{:S(2)}) %all-to-all-start.3) | async-done | bytes 1048608 | tf_op jit(solution)/shard_map/all_to_all | solution.py:233
  82.8 1.1 %shard_map.133 = bf16[128,4096]{1,0:T(8,128)(2,1)} custom-call(bf16[4,128,1024]{2,1,0:T(8,128)(2,1)S(1)} %all-to-all-done.3.refs_0_), custom_call_target="tpu_custom_call" | custom-call | bytes 2097152 | tf_op jit(solution)/shard_map/pallas_call | solution.py:155
  (30 shorter events, 1.0 us)
Async XLA Ops:
  0.6 11.6 %copy-start = (bf16[1,128,4096]{2,1,0:T(8,128)(2,1)S(1)}, bf16[1,128,4096]{2,1,0:T(8,128)(2,1)}, u32[]{:S(2)}) copy-start(bf16[1,128,4096]{2,1,0:T(8,128)(2,1)} %param.9) | copy-start | bytes 3145732
  0.6 1.1 %copy-start.1 = (f32[1,1,256,512]{3,2,1,0:T(8,128)S(1)}, f32[1,1,256,512]{3,2,1,0:T(8,128)}, u32[]{:S(2)}) copy-start(f32[1,1,256,512]{3,2,1,0:T(8,128)} %param.15) | copy-start | bytes 1572868
  2.5 9.8 %copy-start.2 = (bf16[1,128,512]{2,1,0:T(8,128)(2,1)S(1)}, bf16[1,128,512]{2,1,0:T(8,128)(2,1)}, u32[]{:S(2)}) copy-start(bf16[1,128,512]{2,1,0:T(8,128)(2,1)} %param.10) | copy-start | bytes 393220
  2.5 24.9 %all-to-all-start = ((bf16[8,32,512]{2,1,0:T(8,128)(2,1)}), bf16[8,32,512]{2,1,0:T(8,128)(2,1)S(1)}, u32[]{:S(2)}, u32[]{:S(2)}) async-start(bf16[8,32,512]{2,1,0:T(8,128)(2,1)} %shard_map.128.after), calls=%async_computation | async-start | bytes 524288 | tf_op jit(solution)/shard_map/all_to_all | solution.py:190
  12.3 0.7 copy-start.5
  12.9 1.0 %copy-start.6 = (f32[1,256,512]{2,1,0:T(8,128)S(1)}, f32[1,256,512]{2,1,0:T(8,128)}, u32[]{:S(2)}) copy-start(f32[1,256,512]{2,1,0:T(8,128)} %param.11) | copy-start | bytes 1572868
  14.0 13.4 %copy-start.3 = (f32[1,8,512]{2,1,0:T(8,128)S(1)}, f32[1,8,512]{2,1,0:T(8,128)}, u32[]{:S(2)}) copy-start(f32[1,8,512]{2,1,0:T(8,128)} %param.16) | copy-start | bytes 49156
  14.0 13.4 %copy-start.4 = (f32[1,8,512]{2,1,0:T(8,128)S(1)}, f32[1,8,512]{2,1,0:T(8,128)}, u32[]{:S(2)}) copy-start(f32[1,8,512]{2,1,0:T(8,128)} %param.17) | copy-start | bytes 49156
  14.0 13.4 %collective-permute-start = (bf16[256,512]{1,0:T(8,128)(2,1)S(1)}, bf16[256,512]{1,0:T(8,128)(2,1)S(1)}, u32[]{:S(2)}, u32[]{:S(2)}) collective-permute-start(bf16[256,512]{1,0:T(8,128)(2,1)S(1)} %convert_element_type.15.refs_1_), channel_id=1, source_target_pairs={{0,2},{1,3},{2,0},{3,1},{4,6},{5,7},{6,4},{7,5},{8,10},{9,11},{10,... | collective-permute-start | bytes 786440 | tf_op jit(solution)/shard_map/ppermute | solution.py:203
  16.6 26.2 %collective-permute-start.1 = (bf16[128,1536]{1,0:T(8,128)(2,1)}, bf16[128,1536]{1,0:T(8,128)(2,1)S(1)}, u32[]{:S(2)}, u32[]{:S(2)}) collective-permute-start(bf16[128,1536]{1,0:T(8,128)(2,1)} %get-tuple-element.23), channel_id=1, source_target_pairs={{0,4},{1,5},{2,6},{3,7},{4,8},{5,9},{6,10},{7,11},{8,12},{9,13},{1... | collective-permute-start | bytes 1179656 | tf_op jit(solution)/shard_map/ppermute | solution.py:199
  19.8 23.0 %collective-permute-start.2 = (bf16[128,1536]{1,0:T(8,128)(2,1)S(1)}, bf16[128,1536]{1,0:T(8,128)(2,1)S(1)}, u32[]{:S(2)}, u32[]{:S(2)}) collective-permute-start(bf16[128,1536]{1,0:T(8,128)(2,1)S(1)} %get-tuple-element.24), channel_id=1, source_target_pairs={{0,8},{1,9},{2,10},{3,11},{4,12},{5,13},{6,14},{7,15},{8,0},{9,1},... | collective-permute-start | bytes 1179656 | tf_op jit(solution)/shard_map/ppermute | solution.py:199
  24.4 18.5 %collective-permute-start.3 = (bf16[128,1536]{1,0:T(8,128)(2,1)S(1)}, bf16[128,1536]{1,0:T(8,128)(2,1)S(1)}, u32[]{:S(2)}, u32[]{:S(2)}) collective-permute-start(bf16[128,1536]{1,0:T(8,128)(2,1)S(1)} %get-tuple-element.25), channel_id=1, source_target_pairs={{0,12},{1,13},{2,14},{3,15},{4,0},{5,1},{6,2},{7,3},{8,4},{9,5},{1... | collective-permute-start | bytes 1179656 | tf_op jit(solution)/shard_map/ppermute | solution.py:199
  28.1 23.3 %all-to-all-start.1 = ((bf16[4,48,512]{2,1,0:T(8,128)(2,1)}), bf16[4,48,512]{2,1,0:T(8,128)(2,1)S(1)}, u32[]{:S(2)}, u32[]{:S(2)}) async-start(bf16[4,48,512]{2,1,0:T(8,128)(2,1)} %shard_map.130), calls=%async_computation.1 | async-start | bytes 393216 | tf_op jit(solution)/shard_map/all_to_all | solution.py:213
  42.9 15.3 %collective-permute-start.4 = (bf16[512,512]{1,0:T(8,128)(2,1)S(1)}, bf16[512,512]{1,0:T(8,128)(2,1)S(1)}, u32[]{:S(2)}, u32[]{:S(2)}) collective-permute-start(bf16[512,512]{1,0:T(8,128)(2,1)S(1)} %pad_maximum_fusion), channel_id=1, source_target_pairs={{0,1},{1,0},{2,3},{3,2},{4,5},{5,4},{6,7},{7,6},{8,9},{9,8},{10,11... | collective-permute-start | bytes 1572872 | tf_op jit(solution)/shard_map/ppermute | solution.py:212
  52.2 14.1 %all-to-all-start.2 = ((bf16[8,32,512]{2,1,0:T(8,128)(2,1)}), bf16[8,32,512]{2,1,0:T(8,128)(2,1)S(1)}, u32[]{:S(2)}, u32[]{:S(2)}) async-start(bf16[8,32,512]{2,1,0:T(8,128)(2,1)} %get-tuple-element.22.refs_0_), calls=%async_computation.2 | async-start | bytes 524288 | tf_op jit(solution)/shard_map/all_to_all | solution.py:231
  61.4 9.1 %collective-permute-start.5 = (bf16[512,512]{1,0:T(8,128)(2,1)}, bf16[512,512]{1,0:T(8,128)(2,1)S(1)}, u32[]{:S(2)}, u32[]{:S(2)}) collective-permute-start(bf16[512,512]{1,0:T(8,128)(2,1)} %get-tuple-element.29), channel_id=1, source_target_pairs={{0,1},{1,0},{2,3},{3,2},{4,5},{5,4},{6,7},{7,6},{8,9},{9,8},{10,11... | collective-permute-start | bytes 1572872 | tf_op jit(solution)/shard_map/ppermute | solution.py:244
  66.3 16.6 %all-to-all-start.3 = ((bf16[4,128,1024]{2,1,0:T(8,128)(2,1)}), bf16[4,128,1024]{2,1,0:T(8,128)(2,1)S(1)}, u32[]{:S(2)}, u32[]{:S(2)}) async-start(bf16[4,128,1024]{2,1,0:T(8,128)(2,1)} %shard_map.132.refs_4_), calls=%async_computation.3 | async-start | bytes 2097152 | tf_op jit(solution)/shard_map/all_to_all | solution.py:233
  70.5 9.5 %copy-start.8 = (f32[1,256,512]{2,1,0:T(8,128)S(1)}, f32[1,256,512]{2,1,0:T(8,128)}, u32[]{:S(2)}) copy-start(f32[1,256,512]{2,1,0:T(8,128)} %param.13) | copy-start | bytes 1572868
  70.5 9.5 %copy-start.9 = (f32[1,256,512]{2,1,0:T(8,128)S(1)}, f32[1,256,512]{2,1,0:T(8,128)}, u32[]{:S(2)}) copy-start(f32[1,256,512]{2,1,0:T(8,128)} %param.12) | copy-start | bytes 1572868
  70.7 9.3 %copy-start.7 = (f32[1,256,512]{2,1,0:T(8,128)S(1)}, f32[1,256,512]{2,1,0:T(8,128)}, u32[]{:S(2)}) copy-start(f32[1,256,512]{2,1,0:T(8,128)} %param.11) | copy-start | bytes 1572868
  70.7 9.3 %collective-permute-start.6 = (bf16[256,512]{1,0:T(8,128)(2,1)S(1)}, bf16[256,512]{1,0:T(8,128)(2,1)S(1)}, u32[]{:S(2)}, u32[]{:S(2)}) collective-permute-start(bf16[256,512]{1,0:T(8,128)(2,1)S(1)} %get-tuple-element.35), channel_id=1, source_target_pairs={{0,2},{1,3},{2,0},{3,1},{4,6},{5,7},{6,4},{7,5},{8,10},{9,11},{10,... | collective-permute-start | bytes 786440 | tf_op jit(solution)/shard_map/ppermute | solution.py:245
